TPU v7x, 32 devices: a whole 2x2x4 slice. The times are simulated.
32 devices in a mesh: dp: 4 (over y, core), row: 2 (over x), col: 4 (over z).
Axes of the slice: x: 2, y: 2, z: 4, core: 2. Of those that a mesh axis runs over, the one named last changes fastest.
Arguments:
- inputs: bfloat16 [8192, 1024], P(('dp', 'col'), 'row'), may hold values from -6 to 6
- segments: int32 [16, 512], P('dp'), may hold values from 0 to 3, never falling along the last dimension, each value on 1 to 256 neighbouring positions
- cotangent: bfloat16 [8192, 1024], P(('dp', 'col'), 'row'), may hold values from -4 to 4
- w_query: float32 [1024, 2048], P(('row', 'dp'), 'col'), may hold values from -0.1875 to 0.1875
- keyvalue_weight: float32 [2, 1024, 1024], P(None, ('row', 'dp'), 'col'), may hold values from -0.1875 to 0.1875
- w_out: float32 [2048, 1024], P(('col', 'dp'), 'row'), may hold values from -0.5 to 0.5
- w_gate_up: float32 [2, 1024, 3072], P(None, ('row', 'dp'), 'col'), may hold values from -0.1875 to 0.1875
- w_down: float32 [3072, 1024], P(('col', 'dp'), 'row'), may hold values from -0.109375 to 0.109375
- first_query: float32 [1024, 2048], P(('row', 'dp'), 'col'), may hold values from -59.73638 to 59.73638
- keyvalue_first_moment: float32 [2, 1024, 1024], P(None, ('row', 'dp'), 'col'), may hold values from -59.73638 to 59.73638
- first_out: float32 [2048, 1024], P(('col', 'dp'), 'row'), may hold values from -14.934095 to 14.934095
- first_gate_up: float32 [2, 1024, 3072], P(None, ('row', 'dp'), 'col'), may hold values from -20.907734 to 20.907734
- first_down: float32 [3072, 1024], P(('col', 'dp'), 'row'), may hold values from -35.841827 to 35.841827
- second_query: float32 [1024, 2048], P(('row', 'dp'), 'col'), may hold values from 8.192 to 32.768
- keyvalue_second_moment: float32 [2, 1024, 1024], P(None, ('row', 'dp'), 'col'), may hold values from 8.192 to 32.768
- second_out: float32 [2048, 1024], P(('col', 'dp'), 'row'), may hold values from 0.512 to 2.048
- second_gate_up: float32 [2, 1024, 3072], P(None, ('row', 'dp'), 'col'), may hold values from 1.00352 to 4.01408
- second_down: float32 [3072, 1024], P(('col', 'dp'), 'row'), may hold values from 2.94912 to 11.79648
- norm_gains: float32 [2304], replicated, may hold values from 0.4 to 2.4
- gains_first: float32 [2304], replicated, may hold values from -119.47276 to 119.47276
- gains_second: float32 [2304], replicated, may hold values from 32.768 to 131.072
Outputs:
- outputs: float32 [8192, 1024], P(('dp', 'col'), 'row')
- input_grad: float32 [8192, 1024], P(('dp', 'col'), 'row')
- new_query: float32 [1024, 2048], P(('row', 'dp'), 'col')
- new_keyval: float32 [2, 1024, 1024], P(None, ('row', 'dp'), 'col')
- new_out: float32 [2048, 1024], P(('col', 'dp'), 'row')
- new_gate_up: float32 [2, 1024, 3072], P(None, ('row', 'dp'), 'col')
- new_down: float32 [3072, 1024], P(('col', 'dp'), 'row')
- new_first_query: float32 [1024, 2048], P(('row', 'dp'), 'col')
- new_first_keyval: float32 [2, 1024, 1024], P(None, ('row', 'dp'), 'col')
- new_first_out: float32 [2048, 1024], P(('col', 'dp'), 'row')
- new_first_gate_up: float32 [2, 1024, 3072], P(None, ('row', 'dp'), 'col')
- new_first_down: float32 [3072, 1024], P(('col', 'dp'), 'row')
- new_second_query: float32 [1024, 2048], P(('row', 'dp'), 'col')
- new_second_keyval: float32 [2, 1024, 1024], P(None, ('row', 'dp'), 'col')
- new_second_out: float32 [2048, 1024], P(('col', 'dp'), 'row')
- new_second_gate_up: float32 [2, 1024, 3072], P(None, ('row', 'dp'), 'col')
- new_second_down: float32 [3072, 1024], P(('col', 'dp'), 'row')
- new_gains: float32 [2304], replicated
- new_gains_first: float32 [2304], replicated
- new_gains_second: float32 [2304], replicated
All inputs are finite; a program needn't handle non-finite values.
Results may differ from a plain program's by a relative error of at most 0.014.
The roundings to bfloat16 on the way count: a program that leaves them out, or rounds other values in their place, can miss the bound.
Values may be sent and summed in bfloat16 or wider, within the bound.
A program may use at most 128 MiB of HBM per device.

v0:
```python
import jax
import jax.numpy as jnp
from jax import lax
from jax.sharding import PartitionSpec as P

MODEL_WIDTH = 1024
HEAD_SIZE = 128
SEQUENCE_LENGTH = 512
SEQ_DP = 4
STEP = 10


epsilon = 1e-06
rope_base = 1000000.0
masked_score = -1e30
beta_first = 0.9
beta_second = 0.999
learning_rate = 0.05
gains_rate = 0.6
adam_epsilon = 1e-08
weight_decay = 0.1


def rms_scale(values):
    return lax.rsqrt(jnp.mean(values * values, axis=-1, keepdims=True) + epsilon)


def rotate(values, cosine_table, sinus_table):
    half_width = values.shape[-1] // 2
    turned = jnp.concatenate([-values[..., half_width:], values[..., :half_width]], axis=-1)
    return values * cosine_table + turned * sinus_table


def rope_tables(positions):
    exponent = jnp.arange(HEAD_SIZE // 2, dtype=jnp.float32) * (2.0 / HEAD_SIZE)
    inverse = jnp.exp(-jnp.log(jnp.float32(rope_base)) * exponent)
    angles = positions.astype(jnp.float32)[..., None] * inverse
    angles = jnp.concatenate([angles, angles], axis=-1)
    return (jnp.cos(angles), jnp.sin(angles))


def allowed(segment_ids):
    length = segment_ids.shape[-1]
    order = jnp.arange(length)
    causal = order[None, :] <= order[:, None]
    return (segment_ids[..., :, None] == segment_ids[..., None, :]) & causal


def head_slice_part(pre_values, gain_vec, cosine_table, sinus_table):
    return rotate(pre_values * rms_scale(pre_values) * gain_vec, cosine_table, sinus_table)


def row_total(values):
    return lax.psum(values, "row")


def norm_scale(resid):
    return lax.rsqrt(row_total(jnp.sum(resid * resid, axis=-1)) / MODEL_WIDTH + epsilon)[:, None]


def norm_back(grad_normed, resid, scale, gain_vec):
    weighted = grad_normed * gain_vec
    inner = row_total(jnp.sum(weighted * resid, axis=-1))[:, None]
    resid_grad = scale * weighted - resid * (scale * scale * scale) * inner / MODEL_WIDTH
    gain_grad = jnp.sum(grad_normed * resid * scale, axis=0)
    return (resid_grad, gain_grad)


def project_in(normed, block_one, block_two):
    gathered = lax.all_gather(normed, "col", axis=0, tiled=True)
    part_one = jnp.einsum("td,kdf->ktf", gathered, block_one, preferred_element_type=jnp.float32)
    part_two = jnp.einsum("td,kdf->ktf", gathered, block_two, preferred_element_type=jnp.float32)
    sum_one, sum_two = (
        lax.psum_scatter(part_one, "row", scatter_dimension=2, tiled=True),
        lax.psum_scatter(part_two, "row", scatter_dimension=2, tiled=True),
    )
    return (gathered, sum_one, sum_two)


def project_out(values_low, weight_block):
    gathered = lax.all_gather(values_low, "row", axis=1, tiled=True)
    return (
        gathered,
        lax.psum_scatter(
            jnp.dot(gathered, weight_block, preferred_element_type=jnp.float32),
            "col",
            scatter_dimension=0,
            tiled=True,
        ),
    )


def back_out(grad_low, kept, weight_block):
    grad_rows = lax.all_gather(grad_low, "col", axis=0, tiled=True)
    weight_grad = jnp.einsum("tf,td->fd", kept, grad_rows, preferred_element_type=jnp.float32)
    partial_value = jnp.einsum(
        "td,fd->tf", grad_rows, weight_block, preferred_element_type=jnp.float32
    )
    summed = lax.psum_scatter(partial_value, "row", scatter_dimension=1, tiled=True)
    return (weight_grad, summed)


def back_in(grad_one, grad_two, kept_rows, block_one, block_two):
    full_one, full_two = (
        lax.all_gather(grad_one, "row", axis=2, tiled=True),
        lax.all_gather(grad_two, "row", axis=2, tiled=True),
    )
    wgrad_one = jnp.einsum("td,ktf->kdf", kept_rows, full_one, preferred_element_type=jnp.float32)
    wgrad_two = jnp.einsum("td,ktf->kdf", kept_rows, full_two, preferred_element_type=jnp.float32)
    return (
        wgrad_one,
        wgrad_two,
        lax.psum_scatter(
            jnp.einsum("ktf,kdf->td", full_one, block_one, preferred_element_type=jnp.float32)
            + jnp.einsum("ktf,kdf->td", full_two, block_two, preferred_element_type=jnp.float32),
            "col",
            scatter_dimension=0,
            tiled=True,
        ),
    )


def attend_forward(item_set):
    query_matrix, keys_in, values_in, permitted_mask = item_set
    scores = jnp.einsum(
        "qhgd,khd->hgqk", query_matrix, keys_in, preferred_element_type=jnp.float32
    ) * HEAD_SIZE ** (-0.5)
    scores = jnp.where(permitted_mask, scores, masked_score)
    largest = jnp.max(scores, axis=-1, keepdims=True)
    exp_scores = jnp.exp(scores - largest)
    row_sum = jnp.sum(exp_scores, axis=-1, keepdims=True)
    probs_low = (exp_scores / row_sum).astype(jnp.bfloat16)
    blended_output = jnp.einsum(
        "hgqk,khd->qhgd", probs_low, values_in, preferred_element_type=jnp.float32
    )
    return (blended_output, largest + jnp.log(row_sum))


def attend_backward(item_set):
    query_matrix, keys_in, values_in, grad_low, log_total, permitted_mask = item_set
    scores = jnp.einsum(
        "qhgd,khd->hgqk", query_matrix, keys_in, preferred_element_type=jnp.float32
    ) * HEAD_SIZE ** (-0.5)
    scores = jnp.where(permitted_mask, scores, masked_score)
    probs = jnp.exp(scores - log_total)
    prob_grad = jnp.einsum(
        "qhgd,khd->hgqk", grad_low, values_in, preferred_element_type=jnp.float32
    )
    score_grad = probs * (prob_grad - jnp.sum(probs * prob_grad, axis=-1, keepdims=True))
    score_low = score_grad.astype(jnp.bfloat16)
    query_grad = jnp.einsum(
        "hgqk,khd->qhgd", score_low, keys_in, preferred_element_type=jnp.float32
    ) * HEAD_SIZE ** (-0.5)
    key_grad = jnp.einsum(
        "hgqk,qhgd->khd", score_low, query_matrix, preferred_element_type=jnp.float32
    ) * HEAD_SIZE ** (-0.5)
    value_grad = jnp.einsum(
        "hgqk,qhgd->khd", probs.astype(jnp.bfloat16), grad_low, preferred_element_type=jnp.float32
    )
    return (query_grad, key_grad, value_grad)


def adam_update(weight, gradient, first, second, decay, rate):
    first_new = beta_first * first + (1.0 - beta_first) * gradient
    second_new = beta_second * second + (1.0 - beta_second) * gradient * gradient
    first_hat = first_new / (1.0 - beta_first**STEP)
    second_hat = second_new / (1.0 - beta_second**STEP)
    weight_new = weight - rate * (
        first_hat / (jnp.sqrt(second_hat) + adam_epsilon) + decay * weight
    )
    return (weight_new, first_new, second_new)


def shards(
    inputs,
    segments,
    cotangent,
    w_query,
    keyvalue_weight,
    w_out,
    w_gate_up,
    w_down,
    first_query,
    keyvalue_first_moment,
    first_out,
    first_gate_up,
    first_down,
    second_query,
    keyvalue_second_moment,
    second_out,
    second_gate_up,
    second_down,
    norm_gains,
    gains_first,
    gains_second,
):
    query_block, keyval_block, out_block, gate_up_block, down_block = (
        lax.all_gather(w_query.astype(jnp.bfloat16), "dp", axis=0, tiled=True),
        lax.all_gather(keyvalue_weight.astype(jnp.bfloat16), "dp", axis=1, tiled=True),
        lax.all_gather(w_out.astype(jnp.bfloat16), "dp", axis=0, tiled=True),
        lax.all_gather(w_gate_up.astype(jnp.bfloat16), "dp", axis=1, tiled=True),
        lax.all_gather(w_down.astype(jnp.bfloat16), "dp", axis=0, tiled=True),
    )
    tokens_group = SEQ_DP * SEQUENCE_LENGTH
    row_index = lax.axis_index("row")
    width_row = inputs.shape[1]
    gain_attn = lax.dynamic_slice_in_dim(norm_gains, row_index * width_row, width_row)
    gain_mlp = lax.dynamic_slice_in_dim(norm_gains, MODEL_WIDTH + row_index * width_row, width_row)
    gain_query = norm_gains[2 * MODEL_WIDTH : 2 * MODEL_WIDTH + HEAD_SIZE]
    key_norm_gain = norm_gains[2 * MODEL_WIDTH + HEAD_SIZE :]
    permitted_mask = allowed(segments)
    positions = jnp.sum(permitted_mask.astype(jnp.int32), axis=-1) - 1
    cosine_table, sinus_table = rope_tables(positions.reshape(-1))
    cosine_table = cosine_table[:, None, :]
    sinus_table = sinus_table[:, None, :]
    resid_in = inputs.astype(jnp.float32)
    scale_attn = norm_scale(resid_in)
    normed_attn = (resid_in * scale_attn * gain_attn).astype(jnp.bfloat16)
    rows_attn, query_pre, keyvalue_preactivation = project_in(
        normed_attn, query_block[None], keyval_block
    )
    query_heads = query_pre[0].reshape(tokens_group, -1, HEAD_SIZE)
    key_heads = keyvalue_preactivation[0].reshape(tokens_group, -1, HEAD_SIZE)
    kv_count = key_heads.shape[1]
    group_size = query_heads.shape[1] // kv_count
    query_rot, pull_query = jax.vjp(
        lambda pre_values, gain_vec: head_slice_part(
            pre_values, gain_vec, cosine_table, sinus_table
        ),
        query_heads,
        gain_query,
    )
    key_rot, pull_key = jax.vjp(
        lambda pre_values, gain_vec: head_slice_part(
            pre_values, gain_vec, cosine_table, sinus_table
        ),
        key_heads,
        key_norm_gain,
    )
    query_seq = query_rot.astype(jnp.bfloat16).reshape(
        SEQ_DP, SEQUENCE_LENGTH, kv_count, group_size, HEAD_SIZE
    )
    key_seq = key_rot.astype(jnp.bfloat16).reshape(SEQ_DP, SEQUENCE_LENGTH, kv_count, HEAD_SIZE)
    value_seq = (
        keyvalue_preactivation[1]
        .astype(jnp.bfloat16)
        .reshape(SEQ_DP, SEQUENCE_LENGTH, kv_count, HEAD_SIZE)
    )
    attn_mixed, log_total = lax.map(attend_forward, (query_seq, key_seq, value_seq, permitted_mask))
    attn_low = attn_mixed.reshape(tokens_group, -1).astype(jnp.bfloat16)
    heads_all, attn_part = project_out(attn_low, out_block)
    resid_mid = resid_in + attn_part
    scale_mlp = norm_scale(resid_mid)
    normed_mlp = (resid_mid * scale_mlp * gain_mlp).astype(jnp.bfloat16)
    rows_mlp, gate_pre, up_pre = project_in(normed_mlp, gate_up_block[0:1], gate_up_block[1:2])
    gate_vals = gate_pre[0]
    up_vals = up_pre[0]
    sigmoid_gate = jax.nn.sigmoid(gate_vals)
    silu_gate = gate_vals * sigmoid_gate
    hidden_low = (silu_gate * up_vals).astype(jnp.bfloat16)
    hidden_all, mlp_part = project_out(hidden_low, down_block)
    outputs = resid_mid + mlp_part
    down_grad, hidden_grad = back_out(cotangent, hidden_all, down_block)
    gate_grad = (
        hidden_grad * up_vals * sigmoid_gate * (1.0 + gate_vals * (1.0 - sigmoid_gate))
    ).astype(jnp.bfloat16)
    up_grad = (hidden_grad * silu_gate).astype(jnp.bfloat16)
    gate_wgrad, up_wgrad, normed_mlp_grad = back_in(
        gate_grad[None], up_grad[None], rows_mlp, gate_up_block[0:1], gate_up_block[1:2]
    )
    gate_up_grad = jnp.concatenate([gate_wgrad, up_wgrad], axis=0)
    mlp_resid_grad, gain_mlp_grad = norm_back(normed_mlp_grad, resid_mid, scale_mlp, gain_mlp)
    mid_grad = cotangent.astype(jnp.float32) + mlp_resid_grad
    out_wgrad, attn_grad = back_out(mid_grad.astype(jnp.bfloat16), heads_all, out_block)
    attn_grad_seq = attn_grad.astype(jnp.bfloat16).reshape(
        SEQ_DP, SEQUENCE_LENGTH, kv_count, group_size, HEAD_SIZE
    )
    query_grad, key_grad, value_grad = lax.map(
        attend_backward, (query_seq, key_seq, value_seq, attn_grad_seq, log_total, permitted_mask)
    )
    query_pre_grad, gain_query_grad = pull_query(query_grad.reshape(tokens_group, -1, HEAD_SIZE))
    key_pre_grad, gain_key_grad = pull_key(key_grad.reshape(tokens_group, -1, HEAD_SIZE))
    query_send = query_pre_grad.reshape(tokens_group, -1).astype(jnp.bfloat16)[None]
    keyval_send = jnp.stack(
        [key_pre_grad.reshape(tokens_group, -1), value_grad.reshape(tokens_group, -1)]
    ).astype(jnp.bfloat16)
    query_wgrad, keyval_wgrad, normed_attn_grad = back_in(
        query_send, keyval_send, rows_attn, query_block[None], keyval_block
    )
    attn_resid_grad, gain_attn_grad = norm_back(normed_attn_grad, resid_in, scale_attn, gain_attn)
    input_grad = mid_grad + attn_resid_grad
    grad_query, grad_keyval, grad_out, grad_gate_up, grad_down = (
        lax.psum_scatter(query_wgrad[0], "dp", scatter_dimension=0, tiled=True),
        lax.psum_scatter(keyval_wgrad, "dp", scatter_dimension=1, tiled=True),
        lax.psum_scatter(out_wgrad, "dp", scatter_dimension=0, tiled=True),
        lax.psum_scatter(gate_up_grad, "dp", scatter_dimension=1, tiled=True),
        lax.psum_scatter(down_grad, "dp", scatter_dimension=0, tiled=True),
    )
    gain_vector = jnp.zeros((2 * MODEL_WIDTH + 2 * HEAD_SIZE,), jnp.float32)
    gain_vector = lax.dynamic_update_slice_in_dim(
        gain_vector, gain_attn_grad, row_index * width_row, 0
    )
    gain_vector = lax.dynamic_update_slice_in_dim(
        gain_vector, gain_mlp_grad, MODEL_WIDTH + row_index * width_row, 0
    )
    gain_vector = gain_vector.at[2 * MODEL_WIDTH : 2 * MODEL_WIDTH + HEAD_SIZE].add(gain_query_grad)
    gain_vector = gain_vector.at[2 * MODEL_WIDTH + HEAD_SIZE :].add(gain_key_grad)
    gains_grad = lax.psum(gain_vector, ("dp", "row", "col"))
    query_new = adam_update(
        w_query, grad_query, first_query, second_query, weight_decay, learning_rate
    )
    keyval_new = adam_update(
        keyvalue_weight,
        grad_keyval,
        keyvalue_first_moment,
        keyvalue_second_moment,
        weight_decay,
        learning_rate,
    )
    out_new = adam_update(w_out, grad_out, first_out, second_out, weight_decay, learning_rate)
    gate_up_new = adam_update(
        w_gate_up, grad_gate_up, first_gate_up, second_gate_up, weight_decay, learning_rate
    )
    down_new = adam_update(w_down, grad_down, first_down, second_down, weight_decay, learning_rate)
    gains_new = adam_update(norm_gains, gains_grad, gains_first, gains_second, 0.0, gains_rate)
    return (
        outputs,
        input_grad,
        query_new[0],
        keyval_new[0],
        out_new[0],
        gate_up_new[0],
        down_new[0],
        query_new[1],
        keyval_new[1],
        out_new[1],
        gate_up_new[1],
        down_new[1],
        query_new[2],
        keyval_new[2],
        out_new[2],
        gate_up_new[2],
        down_new[2],
        gains_new[0],
        gains_new[1],
        gains_new[2],
    )


def solution(mesh):
    in_specs = (
        P(("dp", "col"), "row"),
        P("dp", None),
        P(("dp", "col"), "row"),
        P(("row", "dp"), "col"),
        P(None, ("row", "dp"), "col"),
        P(("col", "dp"), "row"),
        P(None, ("row", "dp"), "col"),
        P(("col", "dp"), "row"),
        P(("row", "dp"), "col"),
        P(None, ("row", "dp"), "col"),
        P(("col", "dp"), "row"),
        P(None, ("row", "dp"), "col"),
        P(("col", "dp"), "row"),
        P(("row", "dp"), "col"),
        P(None, ("row", "dp"), "col"),
        P(("col", "dp"), "row"),
        P(None, ("row", "dp"), "col"),
        P(("col", "dp"), "row"),
        P(),
        P(),
        P(),
    )
    out_specs = (
        P(("dp", "col"), "row"),
        P(("dp", "col"), "row"),
        P(("row", "dp"), "col"),
        P(None, ("row", "dp"), "col"),
        P(("col", "dp"), "row"),
        P(None, ("row", "dp"), "col"),
        P(("col", "dp"), "row"),
        P(("row", "dp"), "col"),
        P(None, ("row", "dp"), "col"),
        P(("col", "dp"), "row"),
        P(None, ("row", "dp"), "col"),
        P(("col", "dp"), "row"),
        P(("row", "dp"), "col"),
        P(None, ("row", "dp"), "col"),
        P(("col", "dp"), "row"),
        P(None, ("row", "dp"), "col"),
        P(("col", "dp"), "row"),
        P(),
        P(),
        P(),
    )
    return jax.shard_map(shards, mesh=mesh, in_specs=in_specs, out_specs=out_specs, check_vma=False)
```

profile of v0, /device:TPU:0, one launch (start us, length us, event | category | flops | bytes accessed | tf_op | source)
XLA Modules:
  0.0 1532.4 jit_solution(15879534038675639721)
XLA Ops:
  26.3 40.1 %all-gather.14.cloned.1.call-done = bf16[2048,512]{1,0:T(8,128)(2,1)} async-done(((bf16[512,512]{1,0:T(8,128)(2,1)}), bf16[2048,512]{1,0:T(8,128)(2,1)}) %all-gather.14.cloned.1.call-update) | async-done | bytes 2097168 | tf_op jit(solution)/shard_map/all_gather | solution.py:70
  95.5 28.9 %reduce-scatter.18.cloned.1.call-done = f32[1,2048,256]{2,1,0:T(8,128)} async-done(((f32[1,2048,512]{2,1,0:T(8,128)}), f32[1,2048,256]{2,1,0:T(8,128)}) %reduce-scatter.18.cloned.1.call-update) | async-done | bytes 2097168 | tf_op jit(solution)/shard_map/reduce_scatter | solution.py:74
  144.1 37.0 %reduce-scatter.16.cloned.1.call-done = f32[2,2048,128]{2,1,0:T(8,128)} async-done(((f32[2,2048,256]{2,1,0:T(8,128)}), f32[2,2048,128]{2,1,0:T(8,128)}) %reduce-scatter.16.cloned.1.call-update) | async-done | bytes 2097168 | tf_op jit(solution)/shard_map/reduce_scatter | solution.py:75
  221.4 26.0 %all-gather.16.cloned.1.call-done = bf16[2048,512]{1,0:T(8,128)(2,1)} async-done(((bf16[2048,256]{1,0:T(8,128)(2,1)}), bf16[2048,512]{1,0:T(8,128)(2,1)}) %all-gather.16.cloned.1.call-update) | async-done | bytes 2097168 | tf_op jit(solution)/shard_map/all_gather | solution.py:81
  254.5 74.8 %reduce-scatter.20.cloned.1.call-done = f32[512,512]{1,0:T(8,128)} async-done(((f32[2048,512]{1,0:T(8,128)}), f32[512,512]{1,0:T(8,128)}) %reduce-scatter.20.cloned.1.call-update) | async-done | bytes 1048592 | tf_op jit(solution)/shard_map/reduce_scatter | solution.py:84
  346.7 30.5 %all-gather.24.cloned.1.call-done = bf16[2048,512]{1,0:T(8,128)(2,1)} async-done(((bf16[512,512]{1,0:T(8,128)(2,1)}), bf16[2048,512]{1,0:T(8,128)(2,1)}) %all-gather.24.cloned.1.call-update) | async-done | bytes 2097168 | tf_op jit(solution)/shard_map/all_gather | solution.py:94
  397.9 48.2 %all-gather.18.cloned.1.call-done = bf16[2048,512]{1,0:T(8,128)(2,1)} async-done(((bf16[512,512]{1,0:T(8,128)(2,1)}), bf16[2048,512]{1,0:T(8,128)(2,1)}) %all-gather.18.cloned.1.call-update) | async-done | bytes 2097168 | tf_op jit(solution)/shard_map/all_gather | solution.py:70
  459.4 64.9 %reduce-scatter.28.cloned.1.call-done = f32[2048,384]{1,0:T(8,128)} async-done(((f32[2048,768]{1,0:T(8,128)}), f32[2048,384]{1,0:T(8,128)}) %reduce-scatter.28.cloned.1.call-update) | async-done | bytes 3145744 | tf_op jit(solution)/shard_map/reduce_scatter | solution.py:99
  524.3 79.3 %reduce-scatter.22.cloned.1.call-done = f32[1,2048,384]{2,1,0:T(8,128)} async-done(((f32[1,2048,768]{2,1,0:T(8,128)}), f32[1,2048,384]{2,1,0:T(8,128)}) %reduce-scatter.22.cloned.1.call-update) | async-done | bytes 3145744 | tf_op jit(solution)/shard_map/reduce_scatter | solution.py:74
  603.5 79.5 %reduce-scatter.24.cloned.1.call-done = f32[1,2048,384]{2,1,0:T(8,128)} async-done(((f32[1,2048,768]{2,1,0:T(8,128)}), f32[1,2048,384]{2,1,0:T(8,128)}) %reduce-scatter.24.cloned.1.call-update) | async-done | bytes 3145744 | tf_op jit(solution)/shard_map/reduce_scatter | solution.py:75
  690.5 43.7 %all-gather.32.cloned.1.call-done = bf16[2048,768]{1,0:T(8,128)(2,1)} async-done(((bf16[2048,384]{1,0:T(8,128)(2,1)}), bf16[2048,768]{1,0:T(8,128)(2,1)}) %all-gather.32.cloned.1.call-update) | async-done | bytes 3145744 | tf_op jit(solution)/shard_map/all_gather | solution.py:105
  740.1 40.6 %all-gather.34.cloned.1.call-done = bf16[2048,768]{1,0:T(8,128)(2,1)} async-done(((bf16[2048,384]{1,0:T(8,128)(2,1)}), bf16[2048,768]{1,0:T(8,128)(2,1)}) %all-gather.34.cloned.1.call-update) | async-done | bytes 3145744 | tf_op jit(solution)/shard_map/all_gather | solution.py:106
  788.0 39.1 %all-gather.22.cloned.1.call-done = bf16[2048,768]{1,0:T(8,128)(2,1)} async-done(((bf16[2048,384]{1,0:T(8,128)(2,1)}), bf16[2048,768]{1,0:T(8,128)(2,1)}) %all-gather.22.cloned.1.call-update) | async-done | bytes 3145744 | tf_op jit(solution)/shard_map/all_gather | solution.py:81
  833.0 73.0 %reduce-scatter.30.cloned.1.call-done = f32[512,512]{1,0:T(8,128)} async-done(((f32[2048,512]{1,0:T(8,128)}), f32[512,512]{1,0:T(8,128)}) %reduce-scatter.30.cloned.1.call-update) | async-done | bytes 1048592 | tf_op jit(solution)/shard_map/reduce_scatter | solution.py:113
  912.7 72.8 %reduce-scatter.26.cloned.1.call-done = f32[512,512]{1,0:T(8,128)} async-done(((f32[2048,512]{1,0:T(8,128)}), f32[512,512]{1,0:T(8,128)}) %reduce-scatter.26.cloned.1.call-update) | async-done | bytes 1048592 | tf_op jit(solution)/shard_map/reduce_scatter | solution.py:84
  989.0 46.6 %all-gather.26.cloned.1.call-done = bf16[2048,512]{1,0:T(8,128)(2,1)} async-done(((bf16[512,512]{1,0:T(8,128)(2,1)}), bf16[2048,512]{1,0:T(8,128)(2,1)}) %all-gather.26.cloned.1.call-update) | async-done | bytes 2097168 | tf_op jit(solution)/shard_map/all_gather | solution.py:94
  1048.6 45.1 %reduce-scatter.32.cloned.1.call-done = f32[2048,256]{1,0:T(8,128)} async-done(((f32[2048,512]{1,0:T(8,128)}), f32[2048,256]{1,0:T(8,128)}) %reduce-scatter.32.cloned.1.call-update) | async-done | bytes 2097168 | tf_op jit(solution)/shard_map/reduce_scatter | solution.py:99
  1096.5 61.9 %while.29 = (s32[]{:T(128)}, f32[4,512,1,2,128]{4,1,0,3,2:T(8,128)}, f32[4,512,1,128]{3,1,0,2:T(8,128)}, bf16[4,512,1,128]{1,3,2,0:T(8,128)(2,1)}, bf16[4,512,1,...) while((s32[]{:T(128)}, ...), condition=%wide.region_24.25_spmd, body=%wide.region_22.24_spmd.sunk | while | flops 676002816 | bytes 33185488 | solution.py:278
  1211.7 30.7 %all-gather.28.cloned.1.call-done = bf16[1,2048,512]{1,2,0:T(8,128)(2,1)} async-done(((bf16[1,2048,256]{1,2,0:T(8,128)(2,1)}), bf16[1,2048,512]{1,2,0:T(8,128)(2,1)}) %all-gather.28.cloned.1.call-update) | async-done | bytes 2097168 | tf_op jit(solution)/shard_map/all_gather | solution.py:105
  1275.6 38.2 %reduce-scatter.42.cloned.1.call-done = f32[2,128,768]{1,2,0:T(8,128)} async-done(((f32[2,512,768]{1,2,0:T(8,128)}), f32[2,128,768]{1,2,0:T(8,128)}) %reduce-scatter.42.cloned.1.call-update) | async-done | bytes 786448 | tf_op jit(solution)/shard_map/reduce_scatter | solution.py:296
  1345.1 23.6 %reduce-scatter.38.cloned.1.call-done = f32[2,128,256]{1,2,0:T(8,128)} async-done(((f32[2,512,256]{1,2,0:T(8,128)}), f32[2,128,256]{1,2,0:T(8,128)}) %reduce-scatter.38.cloned.1.call-update) | async-done | bytes 262160 | tf_op jit(solution)/shard_map/reduce_scatter | solution.py:294
  1372.4 23.9 %reduce-scatter.36.cloned.1.call-done = f32[128,512]{0,1:T(8,128)} async-done(((f32[512,512]{0,1:T(8,128)}), f32[128,512]{0,1:T(8,128)}) %reduce-scatter.36.cloned.1.call-update) | async-done | bytes 262160 | tf_op jit(solution)/shard_map/reduce_scatter | solution.py:293
  1400.0 75.2 %reduce-scatter.34.cloned.1.call-done = f32[512,512]{1,0:T(8,128)} async-done(((f32[2048,512]{1,0:T(8,128)}), f32[512,512]{1,0:T(8,128)}) %reduce-scatter.34.cloned.1.call-update) | async-done | bytes 1048592 | tf_op jit(solution)/shard_map/reduce_scatter | solution.py:113
  1477.7 40.9 %psum.39 = f32[2304]{0:T(1024)S(1)} all-reduce(f32[2304]{0:T(1024)S(1)} %fusion.97), channel_id=1, replica_groups=mesh['dp'=4,'row'=2,'col'=4] {'dp','row','col'}, use_global_device_ids=true, to_apply=%region_39.40 | all-reduce | flops 2304 | bytes 18432 | tf_op jit(solution)/shard_map/psum | solution.py:308
  (420 shorter events, 432.9 us)
Async XLA Ops:
  18.4 105.9 %reduce-scatter.18.cloned.1.call-start = ((), (), s32[]{:S(2)}) async-start(), calls=%async_computation.17 | async-start | bytes 6291456 | tf_op jit(solution)/shard_map/reduce_scatter | solution.py:74
  71.2 109.9 %reduce-scatter.16.cloned.1.call-start = ((), (), s32[]{:S(2)}) async-start(), calls=%async_computation.16 | async-start | bytes 6291456 | tf_op jit(solution)/shard_map/reduce_scatter | solution.py:75
  83.4 164.1 %all-gather.16.cloned.1.call-start = ((), (), s32[]{:S(2)}) async-start(), calls=%async_computation.18 | async-start | bytes 3145728 | tf_op jit(solution)/shard_map/all_gather | solution.py:81
  214.2 115.0 %reduce-scatter.20.cloned.1.call-start = ((), (), s32[]{:S(2)}) async-start(), calls=%async_computation.19 | async-start | bytes 5242880 | tf_op jit(solution)/shard_map/reduce_scatter | solution.py:84
  252.3 124.9 %all-gather.24.cloned.1.call-start = ((), (), s32[]{:S(2)}) async-start(), calls=%async_computation.26 | async-start | bytes 2621440 | tf_op jit(solution)/shard_map/all_gather | solution.py:94
  252.9 144.9 %all-gather.20.cloned.1.call-start = ((), (), s32[]{:S(2)}) async-start(), calls=%async_computation.21 | async-start | bytes 1966080 | tf_op jit(solution)/shard_map/all_gather | solution.py:201
  254.2 191.8 %all-gather.18.cloned.1.call-start = ((), (), s32[]{:S(2)}) async-start(), calls=%async_computation.20 | async-start | bytes 2621440 | tf_op jit(solution)/shard_map/all_gather | solution.py:70
  336.6 187.6 %reduce-scatter.28.cloned.1.call-start = ((), (), s32[]{:S(2)}) async-start(), calls=%async_computation.27 | async-start | bytes 9437184 | tf_op jit(solution)/shard_map/reduce_scatter | solution.py:99
  383.5 220.0 %reduce-scatter.22.cloned.1.call-start = ((), (), s32[]{:S(2)}) async-start(), calls=%async_computation.22 | async-start | bytes 9437184 | tf_op jit(solution)/shard_map/reduce_scatter | solution.py:74
  452.3 230.7 %reduce-scatter.24.cloned.1.call-start = ((), (), s32[]{:S(2)}) async-start(), calls=%async_computation.23 | async-start | bytes 9437184 | tf_op jit(solution)/shard_map/reduce_scatter | solution.py:75
  459.3 274.8 %all-gather.32.cloned.1.call-start = ((), (), s32[]{:S(2)}) async-start(), calls=%async_computation.39 | async-start | bytes 4718592 | tf_op jit(solution)/shard_map/all_gather | solution.py:105
  689.1 91.6 %all-gather.34.cloned.1.call-start = ((), (), s32[]{:S(2)}) async-start(), calls=%async_computation.40 | async-start | bytes 4718592 | tf_op jit(solution)/shard_map/all_gather | solution.py:106
  689.8 137.2 %all-gather.22.cloned.1.call-start = ((), (), s32[]{:S(2)}) async-start(), calls=%async_computation.24 | async-start | bytes 4718592 | tf_op jit(solution)/shard_map/all_gather | solution.py:81
  690.4 215.6 %reduce-scatter.30.cloned.1.call-start = ((), (), s32[]{:S(2)}) async-start(), calls=%async_computation.28 | async-start | bytes 5242880 | tf_op jit(solution)/shard_map/reduce_scatter | solution.py:113
  788.0 197.6 %reduce-scatter.26.cloned.1.call-start = ((), (), s32[]{:S(2)}) async-start(), calls=%async_computation.25 | async-start | bytes 5242880 | tf_op jit(solution)/shard_map/reduce_scatter | solution.py:84
  833.0 202.6 %all-gather.26.cloned.1.call-start = ((), (), s32[]{:S(2)}) async-start(), calls=%async_computation.29 | async-start | bytes 2621440 | tf_op jit(solution)/shard_map/all_gather | solution.py:94
  989.0 104.7 %reduce-scatter.32.cloned.1.call-start = ((), (), s32[]{:S(2)}) async-start(), calls=%async_computation.30 | async-start | bytes 6291456 | tf_op jit(solution)/shard_map/reduce_scatter | solution.py:99
  1040.5 167.3 %all-gather.30.cloned.1.call-start = ((), (), s32[]{:S(2)}) async-start(), calls=%async_computation.32 | async-start | bytes 3145728 | tf_op jit(solution)/shard_map/all_gather | solution.py:106
  1181.9 91.4 %reduce-scatter.44.cloned.1.call-start = ((), (), s32[]{:S(2)}) async-start(), calls=%async_computation.38 | async-start | bytes 1966080 | tf_op jit(solution)/shard_map/reduce_scatter | solution.py:297
  1187.8 126.0 %reduce-scatter.42.cloned.1.call-start = ((), (), s32[]{:S(2)}) async-start(), calls=%async_computation.37 | async-start | bytes 3932160 | tf_op jit(solution)/shard_map/reduce_scatter | solution.py:296
  1195.3 146.1 %reduce-scatter.40.cloned.1.call-start = ((), (), s32[]{:S(2)}) async-start(), calls=%async_computation.36 | async-start | bytes 1310720 | tf_op jit(solution)/shard_map/reduce_scatter | solution.py:295
  1200.0 168.7 %reduce-scatter.38.cloned.1.call-start = ((), (), s32[]{:S(2)}) async-start(), calls=%async_computation.35 | async-start | bytes 1310720 | tf_op jit(solution)/shard_map/reduce_scatter | solution.py:294
  1211.6 184.7 %reduce-scatter.36.cloned.1.call-start = ((), (), s32[]{:S(2)}) async-start(), calls=%async_computation.34 | async-start | bytes 1310720 | tf_op jit(solution)/shard_map/reduce_scatter | solution.py:293
  1246.3 229.0 %reduce-scatter.34.cloned.1.call-start = ((), (), s32[]{:S(2)}) async-start(), calls=%async_computation.33 | async-start | bytes 5242880 | tf_op jit(solution)/shard_map/reduce_scatter | solution.py:113
  (80 other events, 2010.7 us)
Sparse Core Ops, SparseCore 0:
  18.5 47.7 all-gather.13
  71.3 52.9 reduce-scatter.17
  126.8 54.3 reduce-scatter.15
  214.3 33.0 all-gather.15
  252.4 76.7 reduce-scatter.19
  330.7 46.4 all-gather.23
  400.1 45.9 all-gather.17
  448.5 75.7 reduce-scatter.27
  526.4 77.0 reduce-scatter.21
  605.9 77.0 reduce-scatter.23
  689.2 44.9 all-gather.31
  735.7 44.9 all-gather.33
  782.1 44.9 all-gather.21
  829.2 76.7 reduce-scatter.29
  908.3 77.2 reduce-scatter.25
  989.1 46.4 all-gather.25
  1040.6 52.9 reduce-scatter.31
  1174.6 33.0 all-gather.29
  1209.2 33.1 all-gather.27
  1245.1 28.1 reduce-scatter.43
  1275.8 37.9 reduce-scatter.41
  1316.5 24.8 reduce-scatter.39
  1343.8 24.9 reduce-scatter.37
  1398.5 76.7 reduce-scatter.33
  (2 shorter events, 43.1 us)
where the time goes:
time: 1540 us; the launch traced here: 1530 us
  waiting for transfers between devices  1110 us (72%)
  matrix products  121 us (8%)
  local copies, waits for them, and re-layouts  110 us (7%)
  blocking collectives  93.1 us (6%)
  other arithmetic  80.7 us (5%)
    reduce_scatter x2, waiting for transfers between devices, back_in(): lax.psum_scatter(jnp.einsum('ktf,kdf->td', full_one, block_one, preferred...  148 us
    reduce_scatter x2, waiting for transfers between devices, project_out(): lax.psum_scatter(jnp.dot(gathered, weight_block, preferred_element_type=j...  148 us
    reduce_scatter x2, waiting for transfers between devices, project_in(): lax.psum_scatter(part_two, 'row', scatter_dimension=2, tiled=True)  117 us
    reduce_scatter x2, waiting for transfers between devices, back_out(): lax.psum_scatter(partial_value, 'row', scatter_dimension=1, tiled=True)  110 us
    reduce_scatter x2, waiting for transfers between devices, project_in(): lax.psum_scatter(part_one, 'row', scatter_dimension=2, tiled=True)  108 us
    all_gather x2, waiting for transfers between devices, project_in(): gathered = lax.all_gather(normed, 'col', axis=0, tiled=True)  88.2 us
    all_gather x2, waiting for transfers between devices, back_out(): grad_rows = lax.all_gather(grad_low, 'col', axis=0, tiled=True)  77.1 us
    all_gather x2, waiting for transfers between devices, back_in(): lax.all_gather(grad_one, 'row', axis=2, tiled=True)  74.4 us
  transfers between devices with their start and end apart: 26, of which 26 were waited for; matrix products, arithmetic and copies ran while one was open for 10% of the time, Pallas kernels for 0%

commit v1 on v0

v1 whole, which is shorter than its diff:
```python
import jax
import jax.numpy as jnp
from jax import lax
from jax.experimental import pallas as pl
from jax.experimental.pallas import tpu as pltpu
from jax.sharding import PartitionSpec as P

MODEL_WIDTH = 1024
HEAD_SIZE = 128
STEP = 10


epsilon = 1e-06
rope_base = 1000000.0
masked_score = -1e30
beta_first = 0.9
beta_second = 0.999
learning_rate = 0.05
gains_rate = 0.6
adam_epsilon = 1e-08
weight_decay = 0.1
score_scale = HEAD_SIZE ** (-0.5)


def rms_scale(values):
    return lax.rsqrt(jnp.mean(values * values, axis=-1, keepdims=True) + epsilon)


def rotate(values, cosine_table, sinus_table):
    half_width = values.shape[-1] // 2
    turned = jnp.concatenate([-values[..., half_width:], values[..., :half_width]], axis=-1)
    return values * cosine_table + turned * sinus_table


def rope_tables(positions):
    exponent = jnp.arange(HEAD_SIZE // 2, dtype=jnp.float32) * (2.0 / HEAD_SIZE)
    inverse = jnp.exp(-jnp.log(jnp.float32(rope_base)) * exponent)
    angles = positions.astype(jnp.float32)[..., None] * inverse
    angles = jnp.concatenate([angles, angles], axis=-1)
    return (jnp.cos(angles), jnp.sin(angles))


def allowed(segment_ids):
    length = segment_ids.shape[-1]
    order = jnp.arange(length)
    causal = order[None, :] <= order[:, None]
    return (segment_ids[..., :, None] == segment_ids[..., None, :]) & causal


def head_slice_part(pre_values, gain_vec, cosine_table, sinus_table):
    return rotate(pre_values * rms_scale(pre_values) * gain_vec, cosine_table, sinus_table)


def swap_row(values):
    return lax.ppermute(values, "row", [(0, 1), (1, 0)])


def own_half(values, axis, row_index):
    width = values.shape[axis] // 2
    return lax.dynamic_slice_in_dim(values, row_index * width, width, axis)


def other_half(values, axis, row_index):
    width = values.shape[axis] // 2
    return lax.dynamic_slice_in_dim(values, (1 - row_index) * width, width, axis)


def in_row_order(own, peer, row_index, axis):
    return jnp.where(
        row_index == 0,
        jnp.concatenate([own, peer], axis=axis),
        jnp.concatenate([peer, own], axis=axis),
    )


def exchange_columns(block, row_index):
    peer = swap_row(other_half(block, 1, row_index))
    return in_row_order(own_half(block, 1, row_index)[None], peer[None], row_index, 0)


def return_columns(pieces, row_index):
    own = lax.dynamic_index_in_dim(pieces, row_index, 0, keepdims=False)
    peer = swap_row(lax.dynamic_index_in_dim(pieces, 1 - row_index, 0, keepdims=False))
    return in_row_order(own, peer, row_index, 1)


def block_moves(dp_count):
    half = dp_count // 2
    moves = []
    for row in range(2):
        for place in range(dp_count):
            target = 2 * (2 * (place % half) + row) + place // half
            moves.append((2 * place + row, target))
    return moves


def gather_in(pieces):
    dp_count, col_count = lax.axis_size("dp"), lax.axis_size("col")
    gathered = lax.all_gather(pieces, ("dp", "col"), axis=0, tiled=False)
    rows, columns = pieces.shape[1:]
    gathered = gathered.reshape(dp_count, col_count, 2, rows, columns)
    return gathered.transpose(2, 0, 3, 1, 4).reshape(2 * dp_count * rows, col_count * columns)


def scatter_in(grad):
    dp_count, col_count = lax.axis_size("dp"), lax.axis_size("col")
    rows, columns = grad.shape[0] // (2 * dp_count), grad.shape[1] // col_count
    pieces = grad.reshape(2, dp_count, rows, col_count, columns).transpose(1, 3, 0, 2, 4)
    pieces = pieces.reshape(dp_count * col_count, 2, rows, columns)
    return lax.psum_scatter(pieces, ("dp", "col"), scatter_dimension=0, tiled=False)


def gather_out(shard):
    dp_count, col_count = lax.axis_size("dp"), lax.axis_size("col")
    moved = lax.ppermute(shard, ("dp", "row"), block_moves(dp_count))
    gathered = lax.all_gather(moved, ("dp", "col"), axis=0, tiled=False)
    rows, columns = shard.shape
    gathered = gathered.reshape(dp_count // 2, 2, col_count, rows, columns)
    return gathered.transpose(2, 0, 3, 1, 4).reshape(
        col_count * (dp_count // 2) * rows, 2 * columns
    )


def scatter_out(grad):
    dp_count, col_count = lax.axis_size("dp"), lax.axis_size("col")
    rows, columns = grad.shape[0] // (col_count * (dp_count // 2)), grad.shape[1] // 2
    pieces = grad.reshape(col_count, dp_count // 2, rows, 2, columns).transpose(1, 3, 0, 2, 4)
    pieces = pieces.reshape(dp_count * col_count, rows, columns)
    own = lax.psum_scatter(pieces, ("dp", "col"), scatter_dimension=0, tiled=False)
    back = [(target, source) for source, target in block_moves(dp_count)]
    return lax.ppermute(own, ("dp", "row"), back)


def dot(left, right, contract):
    return lax.dot_general(
        left, right, ((contract[0], contract[1]), ((), ())), preferred_element_type=jnp.float32
    )


def probabilities(query, keys, permitted):
    scores = dot(query, keys, ((1,), (1,))) * score_scale
    scores = jnp.where(permitted, scores, masked_score)
    exp_scores = jnp.exp(scores - jnp.max(scores, axis=-1, keepdims=True))
    return exp_scores / jnp.sum(exp_scores, axis=-1, keepdims=True)


def permitted_of(seg_column, seg_line):
    length = seg_line.shape[1]
    place = lax.broadcasted_iota(jnp.int32, (length, length), 0)
    other = lax.broadcasted_iota(jnp.int32, (length, length), 1)
    return (seg_column[...] == seg_line[...]) & (other <= place)


def attend_forward_kernel(seg_column, seg_line, query, keys, values, mixed):
    permitted = permitted_of(seg_column, seg_line)
    for head in range(query.shape[1] // HEAD_SIZE):
        columns = slice(head * HEAD_SIZE, (head + 1) * HEAD_SIZE)
        probs = probabilities(query[:, columns], keys[...], permitted)
        mixed[:, columns] = dot(
            probs.astype(jnp.bfloat16), values[...], ((1,), (0,))
        ).astype(jnp.bfloat16)


def attend_backward_kernel(
    seg_column, seg_line, query, keys, values, grad, query_grad, key_grad, value_grad
):
    permitted = permitted_of(seg_column, seg_line)
    key_total, value_total = None, None
    for head in range(query.shape[1] // HEAD_SIZE):
        columns = slice(head * HEAD_SIZE, (head + 1) * HEAD_SIZE)
        probs = probabilities(query[:, columns], keys[...], permitted)
        prob_grad = dot(grad[:, columns], values[...], ((1,), (1,)))
        inner = jnp.sum(probs * prob_grad, axis=-1, keepdims=True)
        score_low = (probs * (prob_grad - inner)).astype(jnp.bfloat16)
        query_grad[:, columns] = dot(score_low, keys[...], ((1,), (0,))) * score_scale
        key_part = dot(score_low, query[:, columns], ((0,), (0,)))
        value_part = dot(probs.astype(jnp.bfloat16), grad[:, columns], ((0,), (0,)))
        key_total = key_part if head == 0 else key_total + key_part
        value_total = value_part if head == 0 else value_total + value_part
    key_grad[...] = key_total * score_scale
    value_grad[...] = value_total


def attention_call(kernel, seg_column, seg_line, arrays, outs, kv_count):
    length = seg_column.shape[0]

    def block(array):
        return pl.BlockSpec((length, array.shape[1] // kv_count), lambda head: (0, head))

    return pl.pallas_call(
        kernel,
        grid=(kv_count,),
        in_specs=[
            pl.BlockSpec(seg_column.shape, lambda head: (0, 0)),
            pl.BlockSpec(seg_line.shape, lambda head: (0, 0)),
        ]
        + [block(array) for array in arrays],
        out_specs=[block(out) for out in outs],
        out_shape=list(outs),
        compiler_params=pltpu.CompilerParams(vmem_limit_bytes=48 * 1024 * 1024),
    )(seg_column, seg_line, *arrays)


def norm_back(grad_normed, resid, scale, gain_vec):
    weighted = grad_normed * gain_vec
    inner = jnp.sum(weighted * resid, axis=-1, keepdims=True)
    resid_grad = scale * weighted - resid * (scale * scale * scale) * inner / MODEL_WIDTH
    return resid_grad


def adam_update(weight, gradient, first, second, decay, rate):
    first_new = beta_first * first + (1.0 - beta_first) * gradient
    second_new = beta_second * second + (1.0 - beta_second) * gradient * gradient
    first_hat = first_new / (1.0 - beta_first**STEP)
    second_hat = second_new / (1.0 - beta_second**STEP)
    weight_new = weight - rate * (
        first_hat / (jnp.sqrt(second_hat) + adam_epsilon) + decay * weight
    )
    return (weight_new, first_new, second_new)


def shards(
    inputs,
    segments,
    cotangent,
    w_query,
    keyvalue_weight,
    w_out,
    w_gate_up,
    w_down,
    first_query,
    keyvalue_first_moment,
    first_out,
    first_gate_up,
    first_down,
    second_query,
    keyvalue_second_moment,
    second_out,
    second_gate_up,
    second_down,
    norm_gains,
    gains_first,
    gains_second,
):
    low = jnp.bfloat16
    row_index = lax.axis_index("row")
    tokens = inputs.shape[0]
    width_row = inputs.shape[1]

    query_key_value = jnp.concatenate(
        [
            exchange_columns(block.astype(low), row_index)
            for block in (w_query, keyvalue_weight[0], keyvalue_weight[1])
        ],
        axis=2,
    )
    in_block = gather_in(query_key_value)
    out_block = gather_out(w_out.astype(low))
    gate_up_block = gather_in(
        jnp.concatenate(
            [exchange_columns(w_gate_up[which].astype(low), row_index) for which in (0, 1)],
            axis=2,
        )
    )
    down_block = gather_out(w_down.astype(low))

    gain_attn = norm_gains[:MODEL_WIDTH]
    gain_mlp = norm_gains[MODEL_WIDTH : 2 * MODEL_WIDTH]
    gain_query = norm_gains[2 * MODEL_WIDTH : 2 * MODEL_WIDTH + HEAD_SIZE]
    key_norm_gain = norm_gains[2 * MODEL_WIDTH + HEAD_SIZE :]
    segment = lax.dynamic_index_in_dim(segments, lax.axis_index("col"), 0, keepdims=False)
    seg_column, seg_line = segment[:, None], segment[None, :]
    positions = jnp.sum(allowed(segment).astype(jnp.int32), axis=-1) - 1
    cosine_table, sinus_table = rope_tables(positions)
    cosine_table = cosine_table[:, None, :]
    sinus_table = sinus_table[:, None, :]

    resid_in = in_row_order(inputs, swap_row(inputs), row_index, 1).astype(jnp.float32)
    scale_attn = rms_scale(resid_in)
    normed_attn = (resid_in * scale_attn * gain_attn).astype(low)
    col_count = lax.axis_size("col")
    query_wide = w_query.shape[1] // 2
    key_wide = keyvalue_weight.shape[2] // 2
    projected = dot(normed_attn, in_block, ((1,), (0,))).reshape(tokens, col_count, -1)
    query_heads = projected[:, :, :query_wide].reshape(tokens, -1, HEAD_SIZE)
    key_heads = projected[:, :, query_wide : query_wide + key_wide].reshape(tokens, -1, HEAD_SIZE)
    value_low = projected[:, :, query_wide + key_wide :].reshape(tokens, -1).astype(low)
    kv_count = key_heads.shape[1]

    def normed_heads(pre_values, gain_vec):
        return head_slice_part(pre_values, gain_vec, cosine_table, sinus_table)

    query_rot, pull_query = jax.vjp(normed_heads, query_heads, gain_query)
    key_rot, pull_key = jax.vjp(normed_heads, key_heads, key_norm_gain)
    query_low = query_rot.astype(low).reshape(tokens, -1)
    key_low = key_rot.astype(low).reshape(tokens, -1)
    (attn_low,) = attention_call(
        attend_forward_kernel,
        seg_column,
        seg_line,
        (query_low, key_low, value_low),
        (jax.ShapeDtypeStruct(query_low.shape, low),),
        kv_count,
    )
    attn_part = dot(attn_low, out_block, ((1,), (0,))).astype(low)
    attn_sum = attn_part.astype(jnp.float32) + swap_row(attn_part).astype(jnp.float32)
    resid_mid = resid_in + attn_sum
    scale_mlp = rms_scale(resid_mid)
    normed_mlp = (resid_mid * scale_mlp * gain_mlp).astype(low)
    gate_up = dot(normed_mlp, gate_up_block, ((1,), (0,))).reshape(tokens, col_count, 2, -1)
    gate_vals = gate_up[:, :, 0]
    up_vals = gate_up[:, :, 1]
    sigmoid_gate = jax.nn.sigmoid(gate_vals)
    silu_gate = gate_vals * sigmoid_gate
    hidden_low = (silu_gate * up_vals).astype(low).reshape(tokens, -1)
    mlp_part = dot(hidden_low, down_block, ((1,), (0,)))
    outputs = (
        own_half(resid_mid, 1, row_index)
        + own_half(mlp_part, 1, row_index)
        + swap_row(other_half(mlp_part, 1, row_index).astype(low)).astype(jnp.float32)
    )

    cotangent_full = in_row_order(cotangent, swap_row(cotangent), row_index, 1)
    down_grad = dot(hidden_low, cotangent_full, ((0,), (0,))).astype(low)
    grad_down = scatter_out(down_grad).astype(jnp.float32)
    hidden_grad = dot(cotangent_full, down_block, ((1,), (1,))).reshape(gate_vals.shape)
    gate_grad = hidden_grad * up_vals * sigmoid_gate * (1.0 + gate_vals * (1.0 - sigmoid_gate))
    up_grad = hidden_grad * silu_gate
    gate_up_send = jnp.stack([gate_grad, up_grad], axis=2).astype(low).reshape(tokens, -1)
    mlp_back = dot(gate_up_send, gate_up_block, ((1,), (1,))).astype(low)
    normed_mlp_grad = mlp_back.astype(jnp.float32) + swap_row(mlp_back).astype(jnp.float32)
    gate_up_wgrad = dot(normed_mlp, gate_up_send, ((0,), (0,))).astype(low)
    gate_up_pieces = scatter_in(gate_up_wgrad)
    gate_wide = w_gate_up.shape[2] // 2
    grad_gate_up = jnp.stack(
        [
            return_columns(gate_up_pieces[:, :, :gate_wide], row_index),
            return_columns(gate_up_pieces[:, :, gate_wide:], row_index),
        ]
    ).astype(jnp.float32)

    mid_grad = cotangent_full.astype(jnp.float32) + norm_back(
        normed_mlp_grad, resid_mid, scale_mlp, gain_mlp
    )
    gain_mlp_grad = jnp.sum(normed_mlp_grad * resid_mid * scale_mlp, axis=0)
    mid_low = mid_grad.astype(low)
    attn_grad = dot(mid_low, out_block, ((1,), (1,))).astype(low)
    out_wgrad = dot(attn_low, mid_low, ((0,), (0,))).astype(low)
    grad_out = scatter_out(out_wgrad).astype(jnp.float32)
    query_grad, key_grad, value_grad = attention_call(
        attend_backward_kernel,
        seg_column,
        seg_line,
        (query_low, key_low, value_low, attn_grad),
        (
            jax.ShapeDtypeStruct(query_low.shape, jnp.float32),
            jax.ShapeDtypeStruct(key_low.shape, jnp.float32),
            jax.ShapeDtypeStruct(key_low.shape, jnp.float32),
        ),
        kv_count,
    )
    query_pre_grad, gain_query_grad = pull_query(query_grad.reshape(query_heads.shape))
    key_pre_grad, gain_key_grad = pull_key(key_grad.reshape(key_heads.shape))
    send = jnp.concatenate(
        [
            query_pre_grad.reshape(tokens, col_count, -1).astype(low),
            key_pre_grad.reshape(tokens, col_count, -1).astype(low),
            value_grad.reshape(tokens, col_count, -1).astype(low),
        ],
        axis=2,
    ).reshape(tokens, -1)
    in_wgrad = dot(normed_attn, send, ((0,), (0,))).astype(low)
    in_pieces = scatter_in(in_wgrad)
    grad_query = return_columns(in_pieces[:, :, :query_wide], row_index).astype(jnp.float32)
    grad_keyval = jnp.stack(
        [
            return_columns(in_pieces[:, :, query_wide : query_wide + key_wide], row_index),
            return_columns(in_pieces[:, :, query_wide + key_wide :], row_index),
        ]
    ).astype(jnp.float32)
    attn_back = dot(send, in_block, ((1,), (1,)))
    inner_part = jnp.sum(attn_back * gain_attn * resid_in, axis=-1)
    inner = (inner_part + swap_row(inner_part))[:, None]
    normed_attn_grad = own_half(attn_back, 1, row_index) + swap_row(
        other_half(attn_back, 1, row_index).astype(low)
    ).astype(jnp.float32)
    resid_own = inputs.astype(jnp.float32)
    gain_own = lax.dynamic_slice_in_dim(norm_gains, row_index * width_row, width_row)
    input_grad = (
        own_half(mid_grad, 1, row_index)
        + scale_attn * normed_attn_grad * gain_own
        - resid_own * (scale_attn * scale_attn * scale_attn) * inner / MODEL_WIDTH
    )
    gain_attn_grad = jnp.sum(normed_attn_grad * resid_own * scale_attn, axis=0)
    gain_attn_wide = lax.dynamic_update_slice_in_dim(
        jnp.zeros((MODEL_WIDTH,), jnp.float32), gain_attn_grad, row_index * width_row, 0
    )
    gains_grad = lax.psum(
        jnp.concatenate([gain_attn_wide, 0.5 * gain_mlp_grad, gain_query_grad, gain_key_grad]),
        ("dp", "row", "col"),
    )
    query_new = adam_update(
        w_query, grad_query, first_query, second_query, weight_decay, learning_rate
    )
    keyval_new = adam_update(
        keyvalue_weight,
        grad_keyval,
        keyvalue_first_moment,
        keyvalue_second_moment,
        weight_decay,
        learning_rate,
    )
    out_new = adam_update(w_out, grad_out, first_out, second_out, weight_decay, learning_rate)
    gate_up_new = adam_update(
        w_gate_up, grad_gate_up, first_gate_up, second_gate_up, weight_decay, learning_rate
    )
    down_new = adam_update(w_down, grad_down, first_down, second_down, weight_decay, learning_rate)
    gains_new = adam_update(norm_gains, gains_grad, gains_first, gains_second, 0.0, gains_rate)
    return (
        outputs,
        input_grad,
        query_new[0],
        keyval_new[0],
        out_new[0],
        gate_up_new[0],
        down_new[0],
        query_new[1],
        keyval_new[1],
        out_new[1],
        gate_up_new[1],
        down_new[1],
        query_new[2],
        keyval_new[2],
        out_new[2],
        gate_up_new[2],
        down_new[2],
        gains_new[0],
        gains_new[1],
        gains_new[2],
    )


def solution(mesh):
    in_specs = (
        P(("dp", "col"), "row"),
        P("dp", None),
        P(("dp", "col"), "row"),
        P(("row", "dp"), "col"),
        P(None, ("row", "dp"), "col"),
        P(("col", "dp"), "row"),
        P(None, ("row", "dp"), "col"),
        P(("col", "dp"), "row"),
        P(("row", "dp"), "col"),
        P(None, ("row", "dp"), "col"),
        P(("col", "dp"), "row"),
        P(None, ("row", "dp"), "col"),
        P(("col", "dp"), "row"),
        P(("row", "dp"), "col"),
        P(None, ("row", "dp"), "col"),
        P(("col", "dp"), "row"),
        P(None, ("row", "dp"), "col"),
        P(("col", "dp"), "row"),
        P(),
        P(),
        P(),
    )
    out_specs = (
        P(("dp", "col"), "row"),
        P(("dp", "col"), "row"),
        P(("row", "dp"), "col"),
        P(None, ("row", "dp"), "col"),
        P(("col", "dp"), "row"),
        P(None, ("row", "dp"), "col"),
        P(("col", "dp"), "row"),
        P(("row", "dp"), "col"),
        P(None, ("row", "dp"), "col"),
        P(("col", "dp"), "row"),
        P(None, ("row", "dp"), "col"),
        P(("col", "dp"), "row"),
        P(("row", "dp"), "col"),
        P(None, ("row", "dp"), "col"),
        P(("col", "dp"), "row"),
        P(None, ("row", "dp"), "col"),
        P(("col", "dp"), "row"),
        P(),
        P(),
        P(),
    )
    return jax.shard_map(shards, mesh=mesh, in_specs=in_specs, out_specs=out_specs, check_vma=False)
```

time: 1540 us -> 704 us (0.46)
  waiting for transfers between devices: 1110 us -> 331 us
  matrix products: 121 us -> 56.2 us
  blocking collectives: 93.1 us -> 39.9 us
  starting transfers between devices: 2.35 us -> 39.7 us
  local copies, waits for them, and re-layouts: 110 us -> 143 us
  other arithmetic: 80.7 us -> 51 us
  Pallas kernels: 0 us -> 16.3 us
    reduce_scatter x15 -> x4, waiting for transfers between devices: 741 us -> 134 us  [the longest x2 68.9 us: scatter_in(): lax.psum_scatter(pieces, ('dp', 'col'), scatter_dimension=0, tiled=False)]
    all_gather x11 -> x4, waiting for transfers between devices: 367 us -> 117 us  [the longest x2 70.9 us: gather_out(): gathered = lax.all_gather(moved, ('dp', 'col'), axis=0, tiled=False)]
    ppermute x0 -> x21, waiting for transfers between devices: none -> 79.1 us  [the longest x17 79.1 us: swap_row(): return lax.ppermute(values, 'row', [(0, 1), (1, 0)])]
    dot_general x46 -> x12, matrix products: 121 us -> 56.2 us  [dot(): lax.dot_general(left, right, ((contract[0], contract[1]), ((), ())), pref...]
    reshape x2 -> x12, local copies, waits for them, and re-layouts: 3.15 us -> 67.6 us  [the longest x2 20.3 us: scatter_in(): grad.reshape(2, dp_count, rows, col_count, columns).transpose(1, 3, 0, 2, 4)]
    ppermute x0 -> x21, starting transfers between devices: none -> 39.4 us  [the longest x17 34 us: swap_row(): return lax.ppermute(values, 'row', [(0, 1), (1, 0)])]
    transpose x0 -> x6, local copies, waits for them, and re-layouts: none -> 37.8 us  [the longest x2 18.4 us: gather_in(): gathered.transpose(2, 0, 3, 1, 4)]
    all_gather x4 -> x0, blocking collectives: 31.1 us -> none  [the longest x1 9.01 us: shards(): lax.all_gather(w_down.astype(jnp.bfloat16), 'dp', axis=0, tiled=True)]
  transfers between devices with their start and end apart: 26 -> 29, of which waited for: 26 -> 17; matrix products, arithmetic and copies ran while one was open for 10% -> 25% of each run, Pallas kernels for 0% -> 1%
where the time goes in v1:
time: 704 us; the launch traced here: 693 us
  waiting for transfers between devices  331 us (47%)
  local copies, waits for them, and re-layouts  143 us (20%)
  matrix products  56.2 us (8%)
  other arithmetic  51 us (7%)
  blocking collectives  39.9 us (6%)
  starting transfers between devices  39.7 us (6%)
  Pallas kernels  16.3 us (2%)
  between operations  15.7 us (2%)
    ppermute x17, waiting for transfers between devices, swap_row(): return lax.ppermute(values, 'row', [(0, 1), (1, 0)])  79.1 us
    all_gather x2, waiting for transfers between devices, gather_out(): gathered = lax.all_gather(moved, ('dp', 'col'), axis=0, tiled=False)  70.9 us
    reduce_scatter x2, waiting for transfers between devices, scatter_in(): lax.psum_scatter(pieces, ('dp', 'col'), scatter_dimension=0, tiled=False)  68.9 us
    reduce_scatter x2, waiting for transfers between devices, scatter_out(): lax.psum_scatter(pieces, ('dp', 'col'), scatter_dimension=0, tiled=False)  65.1 us
    dot_general x12, matrix products, dot(): lax.dot_general(left, right, ((contract[0], contract[1]), ((), ())), pref...  56.2 us
    all_gather x2, waiting for transfers between devices, gather_in(): gathered = lax.all_gather(pieces, ('dp', 'col'), axis=0, tiled=False)  46.6 us
    psum x1, blocking collectives, shards(): lax.psum(jnp.concatenate([gain_attn_wide, 0.5 * gain_mlp_grad, gain_query...  39.9 us
    ppermute x17, starting transfers between devices, swap_row(): return lax.ppermute(values, 'row', [(0, 1), (1, 0)])  34 us
  transfers between devices with their start and end apart: 29, of which 17 were waited for; matrix products, arithmetic and copies ran while one was open for 25% of the time, Pallas kernels for 1%

profile of v1, /device:TPU:0, one launch (start us, length us, event | category | flops | bytes accessed | tf_op | source)
XLA Modules:
  0.0 692.6 jit_solution(17828854081296424476)
XLA Ops:
  10.7 11.0 %collective-permute-start.2 = (bf16[128,128]{1,0:T(8,128)(2,1)S(1)}, bf16[128,128]{1,0:T(8,128)(2,1)S(1)}, u32[]{:S(2)}, u32[]{:S(2)}) collective-permute-start(bf16[128,128]{1,0:T(8,128)(2,1)S(1)} %get-tuple-element.98), channel_id=1, source_target_pairs={{0,4},{4,0},{1,5},{5,1},{2,6},{6,2},{3,7},{7,3},{8,12},{12,8},{9,1... | collective-permute-start | bytes 98312 | tf_op jit(solution)/shard_map/ppermute | solution.py:55
  47.8 13.0 %all-gather.11.cloned.1.call-done = bf16[2048,512]{1,0:T(8,128)(2,1)} async-done(((bf16[128,512]{1,0:T(8,128)(2,1)}), bf16[2048,512]{1,0:T(8,128)(2,1)}) %all-gather.11.cloned.1.call-update) | async-done | bytes 2097168 | tf_op jit(solution)/shard_map/all_gather | solution.py:116
  66.5 46.6 %all-gather.9.cloned.1.call-done = bf16[32,128,512]{2,1,0:T(8,128)(2,1)} async-done(((bf16[2,128,512]{2,1,0:T(8,128)(2,1)}), bf16[32,128,512]{2,1,0:T(8,128)(2,1)}) %all-gather.9.cloned.1.call-update) | async-done | bytes 4194320 | tf_op jit(solution)/shard_map/all_gather | solution.py:99
  113.1 7.6 %copy.109 = bf16[2,4,128,4,512]{2,1,0,4,3:T(4,128)(2,1)} copy(bf16[2,4,128,4,512]{4,2,0,3,1:T(8,128)(2,1)} %bitcast.220) | data formatting | bytes 8388608 | tf_op jit(solution)/shard_map/transpose | solution.py:102
  120.7 7.8 %reshape.495 = bf16[1024,2048]{0,1:T(8,128)(2,1)} reshape(bf16[2,4,128,4,512]{2,1,0,4,3:T(4,128)(2,1)} %copy.109) | data formatting | bytes 8388608 | tf_op jit(solution)/shard_map/reshape | solution.py:102
  164.7 24.0 %collective-permute-done.5 = bf16[512,1024]{1,0:T(8,128)(2,1)S(1)} collective-permute-done((bf16[512,1024]{1,0:T(8,128)(2,1)S(1)}, bf16[512,1024]{1,0:T(8,128)(2,1)S(1)}, u32[]{:S(2)}, u32[]{:S(2)}) %collective-permute-start.5) | collective-permute-done | bytes 1048608 | tf_op jit(solution)/shard_map/ppermute | solution.py:55
  191.9 10.8 %copy.118 = bf16[2,4,128,4,768]{2,1,0,4,3:T(4,128)(2,1)} copy(bf16[2,4,128,4,768]{4,2,0,3,1:T(8,128)(2,1)} %bitcast.217) | data formatting | bytes 12582912 | tf_op jit(solution)/shard_map/transpose | solution.py:102
  202.7 11.0 %reshape.502 = bf16[1024,3072]{0,1:T(8,128)(2,1)} reshape(bf16[2,4,128,4,768]{2,1,0,4,3:T(4,128)(2,1)} %copy.118) | data formatting | bytes 12582912 | tf_op jit(solution)/shard_map/reshape | solution.py:102
  213.7 6.5 fusion.33
  239.4 65.1 %reduce-scatter.11.cloned.1.call-done = bf16[1,192,512]{2,1,0:T(8,128)(2,1)} async-done(((bf16[16,192,512]{2,1,0:T(8,128)(2,1)}), bf16[1,192,512]{2,1,0:T(8,128)(2,1)}) %reduce-scatter.11.cloned.1.call-update) | async-done | bytes 196624 | tf_op jit(solution)/shard_map/reduce_scatter | solution.py:129
  310.1 57.8 %all-gather.15.cloned.1.call-done = bf16[3072,512]{1,0:T(8,128)(2,1)} async-done(((bf16[192,512]{1,0:T(8,128)(2,1)}), bf16[3072,512]{1,0:T(8,128)(2,1)}) %all-gather.15.cloned.1.call-update) | async-done | bytes 3145744 | tf_op jit(solution)/shard_map/all_gather | solution.py:116
  367.9 6.8 copy.148
  381.0 7.4 %fusion.9 = (bf16[512,4,1,384]{0,3,1,2:T(8,128)(2,1)S(1)}, bf16[512,4,1,384]{0,3,1,2:T(8,128)(2,1)S(1)}) fusion(f32[512,4,2,384]{0,3,2,1:T(8,128)} %copy-done.8, bf16[4,384,1024]{2,1,0:T(8,128)(2,1)} %dot_general.54, bf16[512,512]{1,0:T(8,128)(2,1)} %param.23, bf16[512,512]{1,0:T(8,128)(2,1)} %collective-permute-done.10, pred[]{:T(512)S(6)} %eq.10), kind=kOutput, calls=%fused_computation.22 | convolution fusion | flops 1625554944 | bytes 13631489 | tf_op jit(solution)/shard_map/dot_general | solution.py:135
  389.0 7.5 %convolution_convert_fusion.6 = bf16[512,1024]{1,0:T(8,128)(2,1)S(1)} fusion(bf16[512,3072]{0,1:T(8,128)(2,1)S(1)} %bitcast.222, bf16[1024,3072]{0,1:T(8,128)(2,1)} %reshape.502), kind=kOutput, calls=%fused_computation.60 | convolution fusion | flops 3221749760 | bytes 10485760 | tf_op jit(solution)/shard_map/dot_general | solution.py:135
  398.0 23.8 %collective-permute-done.11 = bf16[512,1024]{1,0:T(8,128)(2,1)S(1)} collective-permute-done((bf16[512,1024]{1,0:T(8,128)(2,1)S(1)}, bf16[512,1024]{1,0:T(8,128)(2,1)S(1)}, u32[]{:S(2)}, u32[]{:S(2)}) %collective-permute-start.11) | collective-permute-done | bytes 1048608 | tf_op jit(solution)/shard_map/ppermute | solution.py:55
  429.3 10.4 %shard_map.357 = (f32[512,1024]{1,0:T(8,128)}, f32[512,512]{1,0:T(8,128)S(1)}, f32[512,512]{1,0:T(8,128)S(1)}) custom-call(s32[512,1]{1,0:T(8,128)S(1)} %copy.116.seg_column, s32[1,512]{1,0:T(1,128)S(1)} %constant_dynamic-slice_fusion.9.seg_line, bf16[512,1024]{1,0:T(8,128)(2,1)S(1)} %add_convert_fusion.query, bf16[512,512]{1,0:T(8,128)(2,1)S(1)} %copy.138.keys, ...), custom_call_target="tpu_custom_call" | custom-call | tf_op jit(solution)/shard_map/pallas_call | solution.py:190
  471.2 7.9 %reshape.508 = bf16[2,4,128,4,512]{4,3,2,1,0:T(4,128)(2,1)} reshape(bf16[1024,2048]{1,0:T(8,128)(2,1)} %convolution_convert_fusion.2) | data formatting | bytes 8388608 | tf_op jit(solution)/shard_map/reshape | solution.py:108
  486.0 8.0 %convolution_convert_fusion = bf16[1024,3072]{1,0:T(8,128)(2,1)} fusion(bf16[512,3072]{0,1:T(8,128)(2,1)} %bitcast.223, f32[512,1024]{1,0:T(8,128)S(1)} %copy-done.7, f32[1024]{0:T(1024)S(1)} %get-tuple-element.101, f32[512]{0:T(512)S(1)} %get-tuple-element.108), kind=kOutput, calls=%fused_computation.1 | convolution fusion | flops 3225944064 | bytes 11540480 | tf_op jit(solution)/shard_map/dot_general | solution.py:135
  494.0 12.3 %reshape.512 = bf16[2,4,128,4,768]{4,3,2,1,0:T(4,128)(2,1)} reshape(bf16[1024,3072]{1,0:T(8,128)(2,1)} %convolution_convert_fusion) | data formatting | bytes 12582912 | tf_op jit(solution)/shard_map/reshape | solution.py:108
  506.3 6.7 copy.131
  528.8 7.7 %collective-permute-done.9 = bf16[512,512]{1,0:T(8,128)(2,1)} collective-permute-done((bf16[512,512]{1,0:T(8,128)(2,1)}, bf16[512,512]{1,0:T(8,128)(2,1)}, u32[]{:S(2)}, u32[]{:S(2)}) %collective-permute-start.9) | collective-permute-done | bytes 524320 | tf_op jit(solution)/shard_map/ppermute | solution.py:55
  549.4 39.9 %psum.7 = f32[2304]{0:T(1024)S(1)} all-reduce(f32[2304]{0:T(1024)S(1)} %pad_maximum_fusion.6), channel_id=1, replica_groups=mesh['dp'=4,'row'=2,'col'=4] {'dp','row','col'}, use_global_device_ids=true, to_apply=%region_17.18 | all-reduce | flops 2304 | bytes 18432 | tf_op jit(solution)/shard_map/psum | solution.py:398
  594.6 6.3 collective-permute-start.15
  607.0 68.9 %reduce-scatter.9.cloned.1.call-done = bf16[1,2,128,768]{3,2,1,0:T(8,128)(2,1)} async-done(((bf16[16,2,128,768]{3,2,1,0:T(8,128)(2,1)}), bf16[1,2,128,768]{3,2,1,0:T(8,128)(2,1)}) %reduce-scatter.9.cloned.1.call-update) | async-done | bytes 393232 | tf_op jit(solution)/shard_map/reduce_scatter | solution.py:110
  (272 shorter events, 201.8 us)
Async XLA Ops:
  7.2 53.6 %all-gather.11.cloned.1.call-start = ((), (), s32[]{:S(2)}) async-start(), calls=%async_computation.9 | async-start | bytes 2228224 | tf_op jit(solution)/shard_map/all_gather | solution.py:116
  9.7 103.4 %all-gather.9.cloned.1.call-start = ((), (), s32[]{:S(2)}) async-start(), calls=%async_computation.8 | async-start | bytes 4456448 | tf_op jit(solution)/shard_map/all_gather | solution.py:99
  10.7 14.1 %collective-permute-start.2 = (bf16[128,128]{1,0:T(8,128)(2,1)S(1)}, bf16[128,128]{1,0:T(8,128)(2,1)S(1)}, u32[]{:S(2)}, u32[]{:S(2)}) collective-permute-start(bf16[128,128]{1,0:T(8,128)(2,1)S(1)} %get-tuple-element.98), channel_id=1, source_target_pairs={{0,4},{4,0},{1,5},{5,1},{2,6},{6,2},{3,7},{7,3},{8,12},{12,8},{9,1... | collective-permute-start | bytes 98312 | tf_op jit(solution)/shard_map/ppermute | solution.py:55
  21.7 3.9 collective-permute-start.3
  22.8 4.3 collective-permute-start.1
  27.9 164.0 %all-gather.13.cloned.1.call-start = ((), (), s32[]{:S(2)}) async-start(), calls=%async_computation.10 | async-start | bytes 6684672 | tf_op jit(solution)/shard_map/all_gather | solution.py:99
  28.1 4.7 collective-permute-start.6
  30.2 5.7 collective-permute-start.7
  36.7 267.8 %reduce-scatter.11.cloned.1.call-start = ((), (), s32[]{:S(2)}) async-start(), calls=%async_computation.7 | async-start | bytes 3342336 | tf_op jit(solution)/shard_map/reduce_scatter | solution.py:129
  36.8 9.4 %collective-permute-start = (bf16[512,512]{1,0:T(8,128)(2,1)S(1)}, bf16[512,512]{1,0:T(8,128)(2,1)}, u32[]{:S(2)}, u32[]{:S(2)}) collective-permute-start(bf16[512,512]{1,0:T(8,128)(2,1)S(1)} %copy-done.18), channel_id=1, source_target_pairs={{0,4},{4,0},{1,5},{5,1},{2,6},{6,2},{3,7},{7,3},{8,12},{12,8},{9,1... | collective-permute-start | bytes 1572872 | tf_op jit(solution)/shard_map/ppermute | solution.py:55
  162.6 26.1 %collective-permute-start.5 = (bf16[512,1024]{1,0:T(8,128)(2,1)S(1)}, bf16[512,1024]{1,0:T(8,128)(2,1)S(1)}, u32[]{:S(2)}, u32[]{:S(2)}) collective-permute-start(bf16[512,1024]{1,0:T(8,128)(2,1)S(1)} %convolution_convert_fusion.5), channel_id=1, source_target_pairs={{0,4},{4,0},{1,5},{5,1},{2,6},{6,2},{3,7},{7,3},{8,12},{12,8},{9,1... | collective-permute-start | bytes 3145736 | tf_op jit(solution)/shard_map/ppermute | solution.py:55
  164.1 59.9 %collective-permute-start.10 = (bf16[512,512]{1,0:T(8,128)(2,1)}, bf16[512,512]{1,0:T(8,128)(2,1)}, u32[]{:S(2)}, u32[]{:S(2)}) collective-permute-start(bf16[512,512]{1,0:T(8,128)(2,1)} %param.23), channel_id=1, source_target_pairs={{0,4},{4,0},{1,5},{5,1},{2,6},{6,2},{3,7},{7,3},{8,12},{12,8},{9,1... | collective-permute-start | bytes 1572872 | tf_op jit(solution)/shard_map/ppermute | solution.py:55
  239.3 128.6 %all-gather.15.cloned.1.call-start = ((), (), s32[]{:S(2)}) async-start(), calls=%async_computation.11 | async-start | bytes 3342336 | tf_op jit(solution)/shard_map/all_gather | solution.py:116
  310.0 279.2 %reduce-scatter.7.cloned.1.call-start = ((), (), s32[]{:S(2)}) async-start(), calls=%async_computation.5 | async-start | bytes 2228224 | tf_op jit(solution)/shard_map/reduce_scatter | solution.py:129
  396.5 25.4 %collective-permute-start.11 = (bf16[512,1024]{1,0:T(8,128)(2,1)S(1)}, bf16[512,1024]{1,0:T(8,128)(2,1)S(1)}, u32[]{:S(2)}, u32[]{:S(2)}) collective-permute-start(bf16[512,1024]{1,0:T(8,128)(2,1)S(1)} %convolution_convert_fusion.6), channel_id=1, source_target_pairs={{0,4},{4,0},{1,5},{5,1},{2,6},{6,2},{3,7},{7,3},{8,12},{12,8},{9,1... | collective-permute-start | bytes 3145736 | tf_op jit(solution)/shard_map/ppermute | solution.py:55
  450.6 142.2 %reduce-scatter.5.cloned.1.call-start = ((), (), s32[]{:S(2)}) async-start(), calls=%async_computation.4 | async-start | bytes 4456448 | tf_op jit(solution)/shard_map/reduce_scatter | solution.py:110
  484.4 191.6 %reduce-scatter.9.cloned.1.call-start = ((), (), s32[]{:S(2)}) async-start(), calls=%async_computation.6 | async-start | bytes 6684672 | tf_op jit(solution)/shard_map/reduce_scatter | solution.py:110
  521.3 15.2 %collective-permute-start.9 = (bf16[512,512]{1,0:T(8,128)(2,1)}, bf16[512,512]{1,0:T(8,128)(2,1)}, u32[]{:S(2)}, u32[]{:S(2)}) collective-permute-start(bf16[512,512]{1,0:T(8,128)(2,1)} %dynamic-slice_convert_fusion.1), channel_id=1, source_target_pairs={{0,4},{4,0},{1,5},{5,1},{2,6},{6,2},{3,7},{7,3},{8,12},{12,8},{9,1... | collective-permute-start | bytes 1572872 | tf_op jit(solution)/shard_map/ppermute | solution.py:55
  528.1 17.9 %collective-permute-start.12 = (bf16[512,512]{1,0:T(8,128)(2,1)S(1)}, bf16[512,512]{1,0:T(8,128)(2,1)}, u32[]{:S(2)}, u32[]{:S(2)}) collective-permute-start(bf16[512,512]{1,0:T(8,128)(2,1)S(1)} %dynamic-slice_convert_fusion), channel_id=1, source_target_pairs={{0,4},{4,0},{1,5},{5,1},{2,6},{6,2},{3,7},{7,3},{8,12},{12,8},{9,1... | collective-permute-start | bytes 1572872 | tf_op jit(solution)/shard_map/ppermute | solution.py:55
  539.1 6.9 collective-permute-start.13
  594.6 8.5 %collective-permute-start.15 = (bf16[128,128]{1,0:T(8,128)(2,1)S(1)}, bf16[128,128]{1,0:T(8,128)(2,1)S(1)}, u32[]{:S(2)}, u32[]{:S(2)}) collective-permute-start(bf16[128,128]{1,0:T(8,128)(2,1)S(1)} %get-tuple-element.94), channel_id=1, source_target_pairs={{0,4},{4,0},{1,5},{5,1},{2,6},{6,2},{3,7},{7,3},{8,12},{12,8},{9,1... | collective-permute-start | bytes 98312 | tf_op jit(solution)/shard_map/ppermute | solution.py:55
  601.1 4.9 collective-permute-start.14
  677.1 5.2 collective-permute-start.18
  678.6 4.7 collective-permute-start.19
  (52 other events, 1092.3 us)
Sparse Core Ops, SparseCore 0:
  10.8 49.9 all-gather.10
  63.6 49.4 all-gather.8
  116.0 60.3 all-gather.12
  239.5 65.0 reduce-scatter.10
  310.2 57.7 all-gather.14
  450.7 60.2 reduce-scatter.6
  515.4 72.4 reduce-scatter.4
  591.9 84.0 reduce-scatter.8

commit v2 on v1

--- a/solution.py
+++ b/solution.py
@@ -321,7 +321,8 @@
     )
 
     cotangent_full = in_row_order(cotangent, swap_row(cotangent), row_index, 1)
-    down_grad = dot(hidden_low, cotangent_full, ((0,), (0,))).astype(low)
+    hidden_kept, _ = lax.optimization_barrier((hidden_low, down_block))
+    down_grad = dot(hidden_kept, cotangent_full, ((0,), (0,))).astype(low)
     grad_down = scatter_out(down_grad).astype(jnp.float32)
     hidden_grad = dot(cotangent_full, down_block, ((1,), (1,))).reshape(gate_vals.shape)
     gate_grad = hidden_grad * up_vals * sigmoid_gate * (1.0 + gate_vals * (1.0 - sigmoid_gate))

time: 704 us -> 631 us (0.90)
  waiting for transfers between devices: 331 us -> 247 us
  matrix products: 56.2 us -> 65.2 us
  local copies, waits for them, and re-layouts: 143 us -> 151 us
    all_gather x2, waiting for transfers between devices: 70.9 us -> 3.1 us  [gather_out(): gathered = lax.all_gather(moved, ('dp', 'col'), axis=0, tiled=False)]
    reduce_scatter x2, waiting for transfers between devices: 65.1 us -> 0.01 us  [scatter_out(): lax.psum_scatter(pieces, ('dp', 'col'), scatter_dimension=0, tiled=False)]
    reduce_scatter x2, waiting for transfers between devices: 68.9 us -> 102 us  [scatter_in(): lax.psum_scatter(pieces, ('dp', 'col'), scatter_dimension=0, tiled=False)]
    all_gather x2, waiting for transfers between devices: 46.6 us -> 75.4 us  [gather_in(): gathered = lax.all_gather(pieces, ('dp', 'col'), axis=0, tiled=False)]
    ppermute x17, waiting for transfers between devices: 79.1 us -> 66.4 us  [swap_row(): return lax.ppermute(values, 'row', [(0, 1), (1, 0)])]
    dot_general x12, matrix products: 56.2 us -> 65.2 us  [dot(): lax.dot_general(left, right, ((contract[0], contract[1]), ((), ())), pref...]
    unnamed x96 -> x110, local copies, waits for them, and re-layouts: 13.1 us -> 19.9 us
  transfers between devices with their start and end apart: 29 -> 29, of which waited for: 17 -> 18; matrix products, arithmetic and copies ran while one was open for 25% -> 35% of each run, Pallas kernels for 1% -> 3%
where the time goes in v2:
time: 631 us; the launch traced here: 624 us
  waiting for transfers between devices  247 us (39%)
  local copies, waits for them, and re-layouts  151 us (24%)
  matrix products  65.2 us (10%)
  other arithmetic  46.3 us (7%)
  starting transfers between devices  43.2 us (7%)
  blocking collectives  40.2 us (6%)
  Pallas kernels  16 us (3%)
  between operations  15.5 us (2%)
    reduce_scatter x2, waiting for transfers between devices, scatter_in(): lax.psum_scatter(pieces, ('dp', 'col'), scatter_dimension=0, tiled=False)  102 us
    all_gather x2, waiting for transfers between devices, gather_in(): gathered = lax.all_gather(pieces, ('dp', 'col'), axis=0, tiled=False)  75.4 us
    ppermute x17, waiting for transfers between devices, swap_row(): return lax.ppermute(values, 'row', [(0, 1), (1, 0)])  66.4 us
    dot_general x12, matrix products, dot(): lax.dot_general(left, right, ((contract[0], contract[1]), ((), ())), pref...  65.2 us
    psum x1, blocking collectives, shards(): lax.psum(jnp.concatenate([gain_attn_wide, 0.5 * gain_mlp_grad, gain_query...  40.2 us
    ppermute x17, starting transfers between devices, swap_row(): return lax.ppermute(values, 'row', [(0, 1), (1, 0)])  37.7 us
    reshape x2, local copies, waits for them, and re-layouts, scatter_in(): grad.reshape(2, dp_count, rows, col_count, columns).transpose(1, 3, 0, 2, 4)  20.1 us
    unnamed x110, local copies, waits for them, and re-layouts  19.9 us
  transfers between devices with their start and end apart: 29, of which 18 were waited for; matrix products, arithmetic and copies ran while one was open for 35% of the time, Pallas kernels for 3%

profile of v2, /device:TPU:0, one launch (start us, length us, event | category | flops | bytes accessed | tf_op | source)
XLA Modules:
  0.0 624.1 jit_solution(9103865277136991271)
XLA Ops:
  10.8 11.0 %collective-permute-start.2 = (bf16[128,128]{1,0:T(8,128)(2,1)S(1)}, bf16[128,128]{1,0:T(8,128)(2,1)S(1)}, u32[]{:S(2)}, u32[]{:S(2)}) collective-permute-start(bf16[128,128]{1,0:T(8,128)(2,1)S(1)} %get-tuple-element.99), channel_id=1, source_target_pairs={{0,4},{4,0},{1,5},{5,1},{2,6},{6,2},{3,7},{7,3},{8,12},{12,8},{9,1... | collective-permute-start | bytes 98312 | tf_op jit(solution)/shard_map/ppermute | solution.py:55
  29.6 10.5 %collective-permute-start.6 = (bf16[128,384]{1,0:T(8,128)(2,1)S(1)}, bf16[128,384]{1,0:T(8,128)(2,1)S(1)}, u32[]{:S(2)}, u32[]{:S(2)}) collective-permute-start(bf16[128,384]{1,0:T(8,128)(2,1)S(1)} %get-tuple-element.83), channel_id=1, source_target_pairs={{0,4},{4,0},{1,5},{5,1},{2,6},{6,2},{3,7},{7,3},{8,12},{12,8},{9,1... | collective-permute-start | bytes 294920 | tf_op jit(solution)/shard_map/ppermute | solution.py:55
  66.6 46.7 %all-gather.9.cloned.1.call-done = bf16[32,128,512]{2,1,0:T(8,128)(2,1)} async-done(((bf16[2,128,512]{2,1,0:T(8,128)(2,1)}), bf16[32,128,512]{2,1,0:T(8,128)(2,1)}) %all-gather.9.cloned.1.call-update) | async-done | bytes 4194320 | tf_op jit(solution)/shard_map/all_gather | solution.py:99
  113.2 7.6 %copy.109 = bf16[2,4,128,4,512]{2,1,0,4,3:T(4,128)(2,1)} copy(bf16[2,4,128,4,512]{4,2,0,3,1:T(8,128)(2,1)} %bitcast.222) | data formatting | bytes 8388608 | tf_op jit(solution)/shard_map/transpose | solution.py:102
  120.9 7.7 %reshape.495 = bf16[1024,2048]{0,1:T(8,128)(2,1)} reshape(bf16[2,4,128,4,512]{2,1,0,4,3:T(4,128)(2,1)} %copy.109) | data formatting | bytes 8388608 | tf_op jit(solution)/shard_map/reshape | solution.py:102
  165.4 6.9 %copy.148 = bf16[2,2,4,192,512]{4,1,3,0,2:T(2,128)(2,1)} copy(bf16[2,2,4,192,512]{4,3,2,1,0:T(8,128)(2,1)} %bitcast.224) | data formatting | bytes 6291456 | tf_op jit(solution)/shard_map/reshape | solution.py:118
  172.3 6.1 dot_general.54
  178.4 11.3 %collective-permute-done.5 = bf16[512,1024]{1,0:T(8,128)(2,1)} collective-permute-done((bf16[512,1024]{1,0:T(8,128)(2,1)}, bf16[512,1024]{1,0:T(8,128)(2,1)}, u32[]{:S(2)}, u32[]{:S(2)}) %collective-permute-start.5) | collective-permute-done | bytes 1048608 | tf_op jit(solution)/shard_map/ppermute | solution.py:55
  194.5 28.8 %all-gather.13.cloned.1.call-done = bf16[32,128,768]{2,1,0:T(8,128)(2,1)} async-done(((bf16[2,128,768]{2,1,0:T(8,128)(2,1)}), bf16[32,128,768]{2,1,0:T(8,128)(2,1)}) %all-gather.13.cloned.1.call-update) | async-done | bytes 6291472 | tf_op jit(solution)/shard_map/all_gather | solution.py:99
  223.3 10.8 %copy.118 = bf16[2,4,128,4,768]{2,1,0,4,3:T(4,128)(2,1)} copy(bf16[2,4,128,4,768]{4,2,0,3,1:T(8,128)(2,1)} %bitcast.217) | data formatting | bytes 12582912 | tf_op jit(solution)/shard_map/transpose | solution.py:102
  234.0 11.0 %reshape.502 = bf16[1024,3072]{0,1:T(8,128)(2,1)} reshape(bf16[2,4,128,4,768]{2,1,0,4,3:T(4,128)(2,1)} %copy.118) | data formatting | bytes 12582912 | tf_op jit(solution)/shard_map/reshape | solution.py:102
  245.0 16.9 %fusion.33 = f32[512,4,2,384]{0,3,2,1:T(8,128)S(1)} fusion(bf16[4,2,384,1024]{3,2,1,0:T(8,128)(2,1)} %bitcast.218, f32[512,1024]{1,0:T(8,128)} %get-tuple-element.55, f32[1024]{0:T(1024)S(1)} %get-tuple-element.102, f32[512]{0:T(512)S(1)} %get-tuple-element.109), kind=kOutput, calls=%fused_computation.78 | convolution fusion | flops 3222798336 | bytes 14686208 | tf_op jit(solution)/shard_map/dot_general | solution.py:135
  262.0 6.5 %fusion.9 = (bf16[512,4,1,384]{0,3,1,2:T(8,128)(2,1)S(1)}, bf16[512,4,1,384]{0,3,1,2:T(8,128)(2,1)S(1)}) fusion(f32[512,4,2,384]{0,3,2,1:T(8,128)S(1)} %fusion.33, bf16[4,384,1024]{2,1,0:T(8,128)(2,1)S(1)} %copy-done.25, bf16[512,512]{1,0:T(8,128)(2,1)} %param.23, bf16[512,512]{1,0:T(8,128)(2,1)} %collective-permute-done.10, pred[]{:T(512)S(6)} %eq.10), kind=kOutput, calls=%fused_computation.22 | convolution fusion | flops 1625554944 | bytes 13631489 | tf_op jit(solution)/shard_map/dot_general | solution.py:135
  274.1 23.9 %collective-permute-done.11 = bf16[512,1024]{1,0:T(8,128)(2,1)S(1)} collective-permute-done((bf16[512,1024]{1,0:T(8,128)(2,1)S(1)}, bf16[512,1024]{1,0:T(8,128)(2,1)S(1)}, u32[]{:S(2)}, u32[]{:S(2)}) %collective-permute-start.11) | collective-permute-done | bytes 1048608 | tf_op jit(solution)/shard_map/ppermute | solution.py:55
  327.6 6.2 reshape.514
  342.3 10.2 %shard_map.357 = (f32[512,1024]{1,0:T(8,128)}, f32[512,512]{1,0:T(8,128)S(1)}, f32[512,512]{1,0:T(8,128)S(1)}) custom-call(s32[512,1]{1,0:T(8,128)S(1)} %copy.116.seg_column, s32[1,512]{1,0:T(1,128)S(1)} %constant_dynamic-slice_fusion.9.seg_line, bf16[512,1024]{1,0:T(8,128)(2,1)S(1)} %add_convert_fusion.query, bf16[512,512]{1,0:T(8,128)(2,1)S(1)} %copy.138.keys, ...), custom_call_target="tpu_custom_call" | custom-call | tf_op jit(solution)/shard_map/pallas_call | solution.py:190
  372.9 7.8 %reshape.508 = bf16[2,4,128,4,512]{4,3,2,1,0:T(4,128)(2,1)} reshape(bf16[1024,2048]{1,0:T(8,128)(2,1)} %convolution_convert_fusion.2) | data formatting | bytes 8388608 | tf_op jit(solution)/shard_map/reshape | solution.py:108
  387.7 7.9 %convolution_convert_fusion = bf16[1024,3072]{1,0:T(8,128)(2,1)} fusion(bf16[512,3072]{0,1:T(8,128)(2,1)} %bitcast.226, f32[512,1024]{1,0:T(8,128)S(1)} %copy-done.7, f32[1024]{0:T(1024)S(1)} %get-tuple-element.102, f32[512]{0:T(512)S(1)} %get-tuple-element.109), kind=kOutput, calls=%fused_computation.1 | convolution fusion | flops 3225944064 | bytes 11540480 | tf_op jit(solution)/shard_map/dot_general | solution.py:135
  395.6 12.3 %reshape.512 = bf16[2,4,128,4,768]{4,3,2,1,0:T(4,128)(2,1)} reshape(bf16[1024,3072]{1,0:T(8,128)(2,1)} %convolution_convert_fusion) | data formatting | bytes 12582912 | tf_op jit(solution)/shard_map/reshape | solution.py:108
  407.9 6.7 %copy.131 = bf16[4,4,2,128,768]{4,3,2,1,0:T(8,128)(2,1)} copy(bf16[4,4,2,128,768]{4,1,3,0,2:T(4,128)(2,1)} %bitcast.204) | data formatting | bytes 12582912 | tf_op jit(solution)/shard_map/transpose | solution.py:108
  429.4 7.8 %collective-permute-done.9 = bf16[512,512]{1,0:T(8,128)(2,1)} collective-permute-done((bf16[512,512]{1,0:T(8,128)(2,1)}, bf16[512,512]{1,0:T(8,128)(2,1)}, u32[]{:S(2)}, u32[]{:S(2)}) %collective-permute-start.9) | collective-permute-done | bytes 524320 | tf_op jit(solution)/shard_map/ppermute | solution.py:55
  449.8 40.2 %psum.7 = f32[2304]{0:T(1024)S(1)} all-reduce(f32[2304]{0:T(1024)S(1)} %pad_maximum_fusion.6), channel_id=1, replica_groups=mesh['dp'=4,'row'=2,'col'=4] {'dp','row','col'}, use_global_device_ids=true, to_apply=%region_17.18 | all-reduce | flops 2304 | bytes 18432 | tf_op jit(solution)/shard_map/psum | solution.py:399
  496.3 23.2 %reduce-scatter.5.cloned.1.call-done = bf16[1,2,128,512]{3,2,1,0:T(8,128)(2,1)} async-done(((bf16[16,2,128,512]{3,2,1,0:T(8,128)(2,1)}), bf16[1,2,128,512]{3,2,1,0:T(8,128)(2,1)}) %reduce-scatter.5.cloned.1.call-update) | async-done | bytes 262160 | tf_op jit(solution)/shard_map/reduce_scatter | solution.py:110
  528.9 78.8 %reduce-scatter.9.cloned.1.call-done = bf16[1,2,128,768]{3,2,1,0:T(8,128)(2,1)} async-done(((bf16[16,2,128,768]{3,2,1,0:T(8,128)(2,1)}), bf16[1,2,128,768]{3,2,1,0:T(8,128)(2,1)}) %reduce-scatter.9.cloned.1.call-update) | async-done | bytes 393232 | tf_op jit(solution)/shard_map/reduce_scatter | solution.py:110
  (288 shorter events, 202.0 us)
Async XLA Ops:
  7.2 53.7 %all-gather.11.cloned.1.call-start = ((), (), s32[]{:S(2)}) async-start(), calls=%async_computation.9 | async-start | bytes 2228224 | tf_op jit(solution)/shard_map/all_gather | solution.py:116
  9.7 103.5 %all-gather.9.cloned.1.call-start = ((), (), s32[]{:S(2)}) async-start(), calls=%async_computation.8 | async-start | bytes 4456448 | tf_op jit(solution)/shard_map/all_gather | solution.py:99
  10.8 14.1 %collective-permute-start.2 = (bf16[128,128]{1,0:T(8,128)(2,1)S(1)}, bf16[128,128]{1,0:T(8,128)(2,1)S(1)}, u32[]{:S(2)}, u32[]{:S(2)}) collective-permute-start(bf16[128,128]{1,0:T(8,128)(2,1)S(1)} %get-tuple-element.99), channel_id=1, source_target_pairs={{0,4},{4,0},{1,5},{5,1},{2,6},{6,2},{3,7},{7,3},{8,12},{12,8},{9,1... | collective-permute-start | bytes 98312 | tf_op jit(solution)/shard_map/ppermute | solution.py:55
  22.8 4.3 collective-permute-start.1
  27.9 137.5 %all-gather.15.cloned.1.call-start = ((), (), s32[]{:S(2)}) async-start(), calls=%async_computation.11 | async-start | bytes 3342336 | tf_op jit(solution)/shard_map/all_gather | solution.py:116
  29.4 193.8 %all-gather.13.cloned.1.call-start = ((), (), s32[]{:S(2)}) async-start(), calls=%async_computation.10 | async-start | bytes 6684672 | tf_op jit(solution)/shard_map/all_gather | solution.py:99
  29.6 13.1 %collective-permute-start.6 = (bf16[128,384]{1,0:T(8,128)(2,1)S(1)}, bf16[128,384]{1,0:T(8,128)(2,1)S(1)}, u32[]{:S(2)}, u32[]{:S(2)}) collective-permute-start(bf16[128,384]{1,0:T(8,128)(2,1)S(1)} %get-tuple-element.83), channel_id=1, source_target_pairs={{0,4},{4,0},{1,5},{5,1},{2,6},{6,2},{3,7},{7,3},{8,12},{12,8},{9,1... | collective-permute-start | bytes 294920 | tf_op jit(solution)/shard_map/ppermute | solution.py:55
  40.2 4.7 collective-permute-start.7
  45.7 444.3 %reduce-scatter.7.cloned.1.call-start = ((), (), s32[]{:S(2)}) async-start(), calls=%async_computation.5 | async-start | bytes 2228224 | tf_op jit(solution)/shard_map/reduce_scatter | solution.py:129
  45.8 10.4 %collective-permute-start = (bf16[512,512]{1,0:T(8,128)(2,1)S(1)}, bf16[512,512]{1,0:T(8,128)(2,1)}, u32[]{:S(2)}, u32[]{:S(2)}) collective-permute-start(bf16[512,512]{1,0:T(8,128)(2,1)S(1)} %copy-done.18), channel_id=1, source_target_pairs={{0,4},{4,0},{1,5},{5,1},{2,6},{6,2},{3,7},{7,3},{8,12},{12,8},{9,1... | collective-permute-start | bytes 1572872 | tf_op jit(solution)/shard_map/ppermute | solution.py:55
  163.4 26.3 %collective-permute-start.5 = (bf16[512,1024]{1,0:T(8,128)(2,1)}, bf16[512,1024]{1,0:T(8,128)(2,1)}, u32[]{:S(2)}, u32[]{:S(2)}) collective-permute-start(bf16[512,1024]{1,0:T(8,128)(2,1)} %convolution_convert_fusion.5), channel_id=1, source_target_pairs={{0,4},{4,0},{1,5},{5,1},{2,6},{6,2},{3,7},{7,3},{8,12},{12,8},{9,1... | collective-permute-start | bytes 3145736 | tf_op jit(solution)/shard_map/ppermute | solution.py:55
  164.9 97.1 %collective-permute-start.10 = (bf16[512,512]{1,0:T(8,128)(2,1)}, bf16[512,512]{1,0:T(8,128)(2,1)}, u32[]{:S(2)}, u32[]{:S(2)}) collective-permute-start(bf16[512,512]{1,0:T(8,128)(2,1)} %param.23), channel_id=1, source_target_pairs={{0,4},{4,0},{1,5},{5,1},{2,6},{6,2},{3,7},{7,3},{8,12},{12,8},{9,1... | collective-permute-start | bytes 1572872 | tf_op jit(solution)/shard_map/ppermute | solution.py:55
  272.5 25.4 %collective-permute-start.11 = (bf16[512,1024]{1,0:T(8,128)(2,1)S(1)}, bf16[512,1024]{1,0:T(8,128)(2,1)S(1)}, u32[]{:S(2)}, u32[]{:S(2)}) collective-permute-start(bf16[512,1024]{1,0:T(8,128)(2,1)S(1)} %convolution_convert_fusion.6), channel_id=1, source_target_pairs={{0,4},{4,0},{1,5},{5,1},{2,6},{6,2},{3,7},{7,3},{8,12},{12,8},{9,1... | collective-permute-start | bytes 3145736 | tf_op jit(solution)/shard_map/ppermute | solution.py:55
  313.3 178.9 %reduce-scatter.11.cloned.1.call-start = ((), (), s32[]{:S(2)}) async-start(), calls=%async_computation.7 | async-start | bytes 3342336 | tf_op jit(solution)/shard_map/reduce_scatter | solution.py:129
  338.1 181.4 %reduce-scatter.5.cloned.1.call-start = ((), (), s32[]{:S(2)}) async-start(), calls=%async_computation.4 | async-start | bytes 4456448 | tf_op jit(solution)/shard_map/reduce_scatter | solution.py:110
  386.1 221.6 %reduce-scatter.9.cloned.1.call-start = ((), (), s32[]{:S(2)}) async-start(), calls=%async_computation.6 | async-start | bytes 6684672 | tf_op jit(solution)/shard_map/reduce_scatter | solution.py:110
  422.0 15.2 %collective-permute-start.9 = (bf16[512,512]{1,0:T(8,128)(2,1)}, bf16[512,512]{1,0:T(8,128)(2,1)}, u32[]{:S(2)}, u32[]{:S(2)}) collective-permute-start(bf16[512,512]{1,0:T(8,128)(2,1)} %dynamic-slice_convert_fusion.1), channel_id=1, source_target_pairs={{0,4},{4,0},{1,5},{5,1},{2,6},{6,2},{3,7},{7,3},{8,12},{12,8},{9,1... | collective-permute-start | bytes 1572872 | tf_op jit(solution)/shard_map/ppermute | solution.py:55
  428.6 17.9 %collective-permute-start.12 = (bf16[512,512]{1,0:T(8,128)(2,1)S(1)}, bf16[512,512]{1,0:T(8,128)(2,1)}, u32[]{:S(2)}, u32[]{:S(2)}) collective-permute-start(bf16[512,512]{1,0:T(8,128)(2,1)S(1)} %dynamic-slice_convert_fusion), channel_id=1, source_target_pairs={{0,4},{4,0},{1,5},{5,1},{2,6},{6,2},{3,7},{7,3},{8,12},{12,8},{9,1... | collective-permute-start | bytes 1572872 | tf_op jit(solution)/shard_map/ppermute | solution.py:55
  439.8 6.6 %collective-permute-start.13 = (f32[512]{0:T(512)S(1)}, f32[512]{0:T(512)S(1)}, u32[]{:S(2)}, u32[]{:S(2)}) collective-permute-start(f32[512]{0:T(512)S(1)} %get-tuple-element.110), channel_id=1, source_target_pairs={{0,4},{4,0},{1,5},{5,1},{2,6},{6,2},{3,7},{7,3},{8,12},{12,8},{9,1... | collective-permute-start | bytes 6152 | tf_op jit(solution)/shard_map/ppermute | solution.py:55
  490.0 4.0 collective-permute-start.17
  521.3 4.0 collective-permute-start.15
  523.4 4.4 collective-permute-start.14
  608.8 5.2 collective-permute-start.18
  610.4 4.7 collective-permute-start.19
  (59 other events, 1287.7 us)
Sparse Core Ops, SparseCore 0:
  10.9 50.0 all-gather.10
  63.7 49.4 all-gather.8
  116.1 43.6 all-gather.14
  162.6 60.6 all-gather.12
  313.4 60.0 reduce-scatter.6
  377.7 65.2 reduce-scatter.10
  447.4 72.0 reduce-scatter.4
  523.4 84.2 reduce-scatter.8
